TPU v7x, 512 devices: a whole 4x4x16 slice. The times are simulated.
512 devices in a mesh: grp: 32 (over z_lo, y), sp: 16 (over z_hi, x, core).
Axes of the slice: x: 4, y: 4, z: 16 (z_hi: 2, z_lo: 8; z = z_hi * 8 + z_lo), core: 2. Of those that a mesh axis runs over, the one named last changes fastest.
Arguments:
- active_qkv: bfloat16 [3, 3072, 6144], P(None, ('grp', 'sp')), may hold values from -8 to 8
- window_kv: bfloat16 [2, 24576, 6144], P(None, 'grp', 'sp'), may hold values from -8 to 8
- slot_owner: int32 [32], replicated, may hold values from 0 to 7, as said below
- oldest_slot: int32 [1], replicated, may hold values from 0 to 7
- timestep: int32 [1], replicated, may hold values from 0 to 49
- time_slopes: float32 [48], replicated, may hold values from 0.02 to 1
- gate_table: float32 [50, 6144], replicated, may hold values from 0.25 to 2
Outputs:
- attended: bfloat16 [3072, 6144], P(('grp', 'sp'))
- new_window: bfloat16 [2, 24576, 6144], P(None, 'grp', 'sp')
Inputs may be any that keep to these rules, and one draw needn't show every extreme that they name: `slot_owner`: each of the 8 slots is held by exactly 4 groups, all in the same half of the groups; a group's slot depends only on its index mod 4 and on its half.
All inputs are finite; a program needn't handle non-finite values.
Results may differ from a plain program's by a relative error of at most 0.018.
Values may be sent and summed in bfloat16 or wider, within the bound.
A program may use at most 64 MiB of HBM per device.

v0:
```python
import math

import jax
import jax.numpy as jnp
from jax import lax
from jax.sharding import PartitionSpec as P

HD = 128
WIN = 8


def body(active_qkv, window_kv, slot_owner, oldest_slot, timestep, time_slopes, gate_table):
    tok_dev = active_qkv.shape[1]
    width = active_qkv.shape[2]
    ways = lax.axis_size("sp")
    groups = lax.axis_size("grp")
    share = width // ways
    local_heads = share // HD
    group_rows = tok_dev * ways
    cache_rows = window_kv.shape[1]
    scale = 1.0 / math.sqrt(HD)
    split = active_qkv.reshape(3, tok_dev, ways, share)
    local = lax.all_to_all(split, "sp", split_axis=2, concat_axis=1, tiled=True).reshape(
        3, group_rows, share
    )
    queries = lax.all_gather(local[0], "grp", axis=0, tiled=True)
    key_rows = jnp.concatenate([window_kv[0], local[1]], axis=0)
    value_rows = jnp.concatenate([window_kv[1], local[2]], axis=0)
    count = cache_rows + group_rows
    group = lax.axis_index("grp")
    oldest = oldest_slot[0]
    group_ids = jnp.arange(groups, dtype=jnp.int32)
    my_slot = jnp.sum(jnp.where(group_ids == group, slot_owner, 0))
    age = (WIN - jnp.mod(my_slot - oldest, WIN)).astype(jnp.float32)
    key_age = jnp.concatenate(
        [jnp.full((cache_rows,), 1.0, jnp.float32) * age, jnp.zeros((group_rows,), jnp.float32)]
    )
    slopes = lax.dynamic_slice_in_dim(time_slopes, lax.axis_index("sp") * local_heads, local_heads)
    bias = slopes[:, None] * key_age[None, :]
    keys_heads = key_rows.reshape(count, local_heads, HD)
    values_heads = value_rows.reshape(count, local_heads, HD)
    per_block = math.gcd(groups, max(1, 512 // group_rows))
    block_rows = per_block * group_rows
    blocks = groups // per_block
    query_blocks = queries.reshape(blocks, block_rows, local_heads, HD)

    def attend(block):
        score = (
            jnp.einsum("qhd,khd->hqk", block, keys_heads, preferred_element_type=jnp.float32)
            * scale
            - bias[:, None, :]
        )
        top = jnp.max(score, axis=2)
        weight = jnp.exp(score - top[..., None])
        total = jnp.sum(weight, axis=2)
        mixed = jnp.einsum(
            "hqk,khd->qhd",
            weight.astype(jnp.bfloat16),
            values_heads,
            preferred_element_type=jnp.float32,
        )
        partial_value = (mixed / jnp.transpose(total)[:, :, None]).astype(jnp.bfloat16)
        return (partial_value.reshape(block_rows, share), jnp.transpose(top + jnp.log(total)))

    partials, spreads = lax.map(attend, query_blocks)
    pieces_out = lax.all_to_all(partials, "grp", split_axis=0, concat_axis=0, tiled=True)
    pieces_lse = lax.all_to_all(spreads, "grp", split_axis=0, concat_axis=0, tiled=True)
    highest = jnp.max(pieces_lse, axis=0)
    factor = jnp.exp(pieces_lse - highest[None])
    denom = jnp.sum(factor, axis=0)
    terms = (
        factor[..., None]
        * pieces_out.reshape(groups, group_rows, local_heads, HD).astype(jnp.float32)
    ).astype(jnp.bfloat16)
    terms = lax.optimization_barrier(terms)
    numer = jnp.sum(terms.astype(jnp.float32), axis=0)
    combined = (numer / denom[..., None]).reshape(group_rows, share).astype(jnp.bfloat16)
    returned = lax.all_to_all(combined, "sp", split_axis=0, concat_axis=1, tiled=True)
    picker = (jnp.arange(gate_table.shape[0], dtype=jnp.int32) == timestep[0]).astype(jnp.float32)
    gate = jnp.dot(picker, gate_table, precision=lax.Precision.HIGHEST)
    attended = (gate[None, :] * returned.astype(jnp.float32)).astype(jnp.bfloat16)
    arrived = lax.all_gather(local[1:], "grp", axis=1, tiled=True)
    is_old = (slot_owner == oldest).astype(jnp.int32)
    before = jnp.sum(jnp.where(group_ids < group, is_old, 0))
    moved = lax.dynamic_slice_in_dim(arrived, before * cache_rows, cache_rows, 1)
    new_window = jnp.where(my_slot == oldest, moved, window_kv)
    return (attended, new_window)


def solution(mesh):
    in_specs = (P(None, ("grp", "sp"), None), P(None, "grp", "sp"), P(), P(), P(), P(), P())
    out_specs = (P(("grp", "sp"), None), P(None, "grp", "sp"))
    return jax.shard_map(body, mesh=mesh, in_specs=in_specs, out_specs=out_specs, check_vma=False)
```

profile of v0, /device:TPU:6, one launch (start us, length us, event | category | flops | bytes accessed | tf_op | source)
XLA Modules:
  0.0 660.9 jit_solution(13535399313655805124)
XLA Ops:
  7.2 1.4 reshape.55
  8.8 33.5 %all_to_all.35 = bf16[3,6,16,384]{3,0,1,2:T(4,128)(2,1)S(1)} all-to-all(bf16[3,6,16,384]{3,0,1,2:T(4,128)(2,1)S(1)} %copy.25), channel_id=1, replica_groups=mesh['grp'=32,'sp'=16] {'sp'}, dimensions={2} | all-to-all | bytes 442368 | tf_op jit(solution)/shard_map/all_to_all | solution.py:23
  42.3 1.8 slice_reduce_fusion
  47.7 1.3 copy.41
  53.3 218.9 %all-gather.3.cloned.1.call-done = bf16[3072,384]{1,0:T(8,128)(2,1)} async-done(((bf16[96,384]{1,0:T(8,128)(2,1)}), bf16[3072,384]{1,0:T(8,128)(2,1)}) %all-gather.3.cloned.1.call-update) | async-done | bytes 2359312 | tf_op jit(solution)/shard_map/all_gather | solution.py:26
  272.1 7.0 %reshape.61 = bf16[32,96,3,128]{3,2,1,0:T(4,128)(2,1)} reshape(bf16[3072,384]{1,0:T(8,128)(2,1)} %all-gather.3.cloned.1.call-done) | data formatting | bytes 4718592 | tf_op jit(solution)/shard_map/reshape | solution.py:45
  279.2 3.8 copy.31
  283.0 93.0 %while.13 = (s32[]{:T(128)}, bf16[32,96,384]{2,1,0:T(8,128)(2,1)}, f32[32,96,3]{1,2,0:T(4,128)S(1)}, bf16[32,96,3,128]{3,1,2,0:T(8,128)(2,1)}, bf16[864,3,128]{2...) while((s32[]{:T(128)}, bf16[32,96,384]{2,1,0:T(8,128)(2,1)}, ...), condition=%wide.region_4.5_spmd.clone, body=%wide.region_1.4_spmd.clone.sunk | while | flops 129219840 | bytes 4940141 | solution.py:65
  286.0 1.3 fusion.34
  309.2 1.3 fusion.34
  315.0 1.3 fusion.34
  317.9 1.3 fusion.34
  320.8 1.3 fusion.34
  323.8 1.3 fusion.34
  332.5 1.3 fusion.34
  335.4 1.3 fusion.34
  347.0 1.3 fusion.34
  355.8 1.3 fusion.34
  358.7 1.3 fusion.34
  361.6 1.3 fusion.34
  364.5 1.3 fusion.34
  370.3 1.3 fusion.34
  373.2 1.3 fusion.34
  376.0 32.0 %all_to_all.36 = f32[32,96,3]{1,2,0:T(4,128)S(1)} all-to-all(f32[32,96,3]{1,2,0:T(4,128)S(1)} %get-tuple-element.40), channel_id=1, replica_groups=mesh['grp'=32,'sp'=16] {'grp'}, dimensions={0} | all-to-all | bytes 73728 | tf_op jit(solution)/shard_map/all_to_all | solution.py:67
  408.1 7.1 %all-to-all-start.2 = ((bf16[32,96,384]{2,1,0:T(8,128)(2,1)}), bf16[32,96,384]{2,1,0:T(8,128)(2,1)}, u32[]{:S(2)}, u32[]{:S(2)}) async-start(bf16[32,96,384]{2,1,0:T(8,128)(2,1)} %get-tuple-element.41), calls=%async_computation.2 | async-start | bytes 4718592 | tf_op jit(solution)/shard_map/all_to_all | solution.py:66
  419.2 87.6 %all-to-all-done.2 = bf16[32,96,384]{2,1,0:T(8,128)(2,1)} async-done(((bf16[32,96,384]{2,1,0:T(8,128)(2,1)}), bf16[32,96,384]{2,1,0:T(8,128)(2,1)}, u32[]{:S(2)}, u32[]{:S(2)}) %all-to-all-start.2) | async-done | bytes 2359328 | tf_op jit(solution)/shard_map/all_to_all | solution.py:66
  506.8 7.4 %reshape.57 = f32[32,96,3,128]{3,2,1,0:T(4,128)} reshape(bf16[32,96,384]{2,1,0:T(8,128)(2,1)} %all-to-all-done.2) | data formatting | bytes 7077888 | tf_op jit(solution)/shard_map/convert_element_type | solution.py:73
  514.2 7.1 %multiply_convert_fusion = bf16[32,96,3,128]{3,2,1,0:T(4,128)(2,1)S(1)} fusion(f32[32,96,3,128]{3,2,1,0:T(4,128)} %reshape.57, f32[32,96,3]{2,1,0:T(8,128)S(1)} %copy.34), kind=kLoop, calls=%fused_computation.18 | loop fusion | flops 2359296 | bytes 7114752 | tf_op jit(solution)/shard_map/convert_element_type | solution.py:74
  521.4 1.4 convert_reduce_fusion
  523.7 7.3 %all-to-all-start.3 = ((bf16[16,6,384]{2,1,0:T(8,128)(2,1)}), bf16[16,6,384]{2,1,0:T(8,128)(2,1)S(1)}, u32[]{:S(2)}, u32[]{:S(2)}) async-start(bf16[16,6,384]{2,1,0:T(8,128)(2,1)} %convert_element_type.50), calls=%async_computation.3 | async-start | bytes 196608 | tf_op jit(solution)/shard_map/all_to_all | solution.py:78
  530.9 118.5 %all-gather.5.cloned.1.call-done = bf16[2,3072,384]{2,0,1:T(2,128)(2,1)} async-done(((bf16[2,96,384]{2,0,1:T(2,128)(2,1)}), bf16[2,3072,384]{2,0,1:T(2,128)(2,1)}) %all-gather.5.cloned.1.call-update) | async-done | bytes 4718608 | tf_op jit(solution)/shard_map/all_gather | solution.py:82
  649.4 2.8 broadcast_select_fusion
  (291 shorter events, 84.1 us)
Async XLA Ops:
  7.2 410.7 %copy-start = (f32[50,6144]{1,0:T(8,128)S(1)}, f32[50,6144]{1,0:T(8,128)}, u32[]{:S(2)}) copy-start(f32[50,6144]{1,0:T(8,128)} %param.15) | copy-start | bytes 3686404
  7.2 38.2 %copy-start.6 = (s32[32]{0:T(128)S(1)}, s32[32]{0:T(128)}, u32[]{:S(2)}) copy-start(s32[32]{0:T(128)} %param.11) | copy-start | bytes 388
  7.2 39.5 %copy-start.1 = (bf16[2,768,384]{2,1,0:T(8,128)(2,1)S(1)}, bf16[2,768,384]{2,1,0:T(8,128)(2,1)}, u32[]{:S(2)}) copy-start(bf16[2,768,384]{2,1,0:T(8,128)(2,1)} %param.10) | copy-start | bytes 3538948
  7.2 264.9 %all-gather.3.cloned.1.call-start = ((), (), s32[]{:S(2)}) async-start(), calls=%async_computation.4 | async-start | bytes 2433024 | tf_op jit(solution)/shard_map/all_gather | solution.py:26
  46.7 3.4 copy-start.7
  47.7 2.5 copy-start.4
  279.2 3.9 copy-start.3
  279.2 3.9 copy-start.5
  408.1 98.7 %all-to-all-start.2 = ((bf16[32,96,384]{2,1,0:T(8,128)(2,1)}), bf16[32,96,384]{2,1,0:T(8,128)(2,1)}, u32[]{:S(2)}, u32[]{:S(2)}) async-start(bf16[32,96,384]{2,1,0:T(8,128)(2,1)} %get-tuple-element.41), calls=%async_computation.2 | async-start | bytes 4718592 | tf_op jit(solution)/shard_map/all_to_all | solution.py:66
  415.2 234.2 %all-gather.5.cloned.1.call-start = ((), (), s32[]{:S(2)}) async-start(), calls=%async_computation.5 | async-start | bytes 4866048 | tf_op jit(solution)/shard_map/all_gather | solution.py:82
  521.4 128.0 %copy-start.2 = (bf16[2,768,384]{2,1,0:T(8,128)(2,1)S(1)}, bf16[2,768,384]{2,1,0:T(8,128)(2,1)}, u32[]{:S(2)}) copy-start(bf16[2,768,384]{2,1,0:T(8,128)(2,1)} %param.10) | copy-start | bytes 3538948
  523.7 129.7 %all-to-all-start.3 = ((bf16[16,6,384]{2,1,0:T(8,128)(2,1)}), bf16[16,6,384]{2,1,0:T(8,128)(2,1)S(1)}, u32[]{:S(2)}, u32[]{:S(2)}) async-start(bf16[16,6,384]{2,1,0:T(8,128)(2,1)} %convert_element_type.50), calls=%async_computation.3 | async-start | bytes 196608 | tf_op jit(solution)/shard_map/all_to_all | solution.py:78
Sparse Core Ops, SparseCore 0:
  44.9 227.2 all-gather.2
  418.7 230.6 all-gather.4
where the time goes:
time: 663 us; the launch traced here: 661 us
  waiting for transfers between devices  425 us (64%)
  blocking collectives  65.6 us (10%)
  local copies, waits for them, and re-layouts  55.3 us (8%)
  matrix products  54.9 us (8%)
  other arithmetic  27.9 us (4%)
  between operations  17.3 us (3%)
  starting transfers between devices  14.5 us (2%)
    all_gather x1, waiting for transfers between devices, body(): queries = lax.all_gather(local[0], 'grp', axis=0, tiled=True)  219 us
    all_gather x1, waiting for transfers between devices, body(): arrived = lax.all_gather(local[1:], 'grp', axis=1, tiled=True)  118 us
    all_to_all x1, waiting for transfers between devices, body(): lax.all_to_all(partials, 'grp', split_axis=0, concat_axis=0, tiled=True)  87.6 us
    dot_general x32, matrix products, attend(): jnp.einsum('qhd,khd->hqk', block, keys_heads, preferred_element_type=jnp....  42.4 us
    all_to_all x1, blocking collectives, body(): lax.all_to_all(split, 'sp', split_axis=2, concat_axis=1, tiled=True)  33.5 us
    all_to_all x1, blocking collectives, body(): lax.all_to_all(spreads, 'grp', split_axis=0, concat_axis=0, tiled=True)  32 us
    dynamic_update_slice x32, local copies, waits for them, and re-layouts, body(): partials, spreads = lax.map(attend, query_blocks)  20.5 us
  transfers between devices with their start and end apart: 4, of which 3 were waited for; matrix products, arithmetic and copies ran while one was open for 5% of the time, Pallas kernels for 0%

commit v1 on v0

v1 whole, which is shorter than its diff:
```python
import functools
import math

import jax
import jax.numpy as jnp
from jax import lax
from jax.experimental import pallas as pl
from jax.experimental.pallas import tpu as pltpu
from jax.sharding import PartitionSpec as P

HD = 128
WIN = 8
HEADS = 3
SHARE = HEADS * HD
ROWS = 96
CACHE = 768
NZ = 8
NY = 4
PACK = 4 * ROWS
LOG2E = math.log2(math.e)
COEF = LOG2E / math.sqrt(HD)
NONE = -1e30
MESH = pl.DeviceIdType.MESH
BF = jnp.bfloat16
F32 = jnp.float32


def lse2(*parts):
    top = functools.reduce(jnp.maximum, parts)
    return top + jnp.log2(sum(jnp.exp2(p - top) for p in parts))


def kernel(
    local_ref, win_ref, bias_ref, out_ref, moved_ref,
    qbuf, vt, va, opart, lpart, lrecv, wrelay, wfinal, zl_own,
    r1, r2, r3, relayed, zo_own, zo_recv, zo_out, zl_recv, zl_out, wz,
    zsend, zrecv, ysend, yrecv, y2send, y2recv,
    ls_sem, lr_sem, r1s, r1r, r2s, r2r, r3s, r3r,
    zos, zor, zls, zlr, ezs, ezr, eys, eyr, e2s, e2r, cp_sem,
):
    me = lax.axis_index("grp")
    z = me // NY
    y = me % NY
    yp = (y + 1) % NY
    ym = (y + 3) % NY
    y2 = (y + 2) % NY
    near = z // 4
    far = 1 - near

    def at(zz, yy):
        return {"grp": zz * NY + yy}

    def copy(src, dst, send, recv, dev):
        return pltpu.make_async_remote_copy(
            src_ref=src, dst_ref=dst, send_sem=send, recv_sem=recv,
            device_id=dev, device_id_type=MESH,
        )

    barrier = pltpu.get_barrier_semaphore()
    for step in range(1, NZ):
        pl.semaphore_signal(barrier, inc=1, device_id=at((z + step) % NZ, y), device_id_type=MESH)
    for step in range(1, NY):
        pl.semaphore_signal(barrier, inc=1, device_id=at(z, (y + step) % NY), device_id_type=MESH)
    pl.semaphore_wait(barrier, NZ - 1 + NY - 1)

    def z_copy(block, side):
        return copy(
            qbuf.at[y, block], qbuf.at[y, block], zsend.at[side, block], zrecv.at[block],
            at(z + 1 - 2 * side, y),
        )

    def y_copy(block, side):
        return copy(
            qbuf.at[y, block], qbuf.at[y, block], ysend.at[side, block], yrecv.at[side, block],
            at(z, ym if side else yp),
        )

    def y2_copy(block, odd):
        column = ym + odd * (yp - ym)
        return copy(
            qbuf.at[column, block], qbuf.at[column, block], y2send.at[block], y2recv.at[block],
            at(z, yp + odd * (ym - yp)),
        )

    def y_wait(block, side):
        column = yp if side else ym
        copy(
            qbuf.at[column, block], qbuf.at[column, block], ysend.at[side, block],
            yrecv.at[side, block], at(z, column),
        ).wait_recv()

    def y2_wait(block):
        copy(
            qbuf.at[y2, block], qbuf.at[y2, block], y2send.at[block], y2recv.at[block], at(z, yp)
        ).wait_recv()

    def z_wait(block):
        copy(
            qbuf.at[y, block], qbuf.at[y, block], zsend.at[0, block], zrecv.at[block], at(z, yp)
        ).wait_recv()

    def spread(block):
        y_copy(block, 0).start()
        y_copy(block, 1).start()

    def evict_z(half):
        rows = pl.ds(((z % 2) * NY + y) * ROWS, ROWS)
        return copy(
            local_ref.at[pl.ds(1, 2)], moved_ref.at[:, rows, :], ezs.at[half], ezr.at[z % 2],
            at(z // 2 + 4 * half, y),
        )

    def evict_own():
        rows = pl.ds(((z % 2) * NY + y) * ROWS, ROWS)
        return pltpu.make_async_copy(
            local_ref.at[pl.ds(1, 2)], moved_ref.at[:, rows, :], cp_sem
        )

    def evict_rows(which, column):
        return moved_ref.at[:, pl.ds((which * NY + column) * ROWS, ROWS), :]

    def evict_y(which, side):
        rows = evict_rows(which, y)
        return copy(
            rows, rows, eys.at[side, which], eyr.at[side, which], at(z, ym if side else yp)
        )

    def evict_y_wait(which, side):
        rows = evict_rows(which, yp if side else ym)
        copy(rows, rows, eys.at[side, which], eyr.at[side, which], at(z, yp)).wait_recv()

    def evict_y2(which):
        rows = evict_rows(which, yp if which else ym)
        return copy(rows, rows, e2s.at[which], e2r.at[which], at(z, ym if which else yp))

    def evict_y2_wait(which):
        rows = evict_rows(which, y2)
        copy(rows, rows, e2s.at[which], e2r.at[which], at(z, yp)).wait_recv()

    qbuf[y, z] = local_ref[0]

    @pl.when(z < NZ - 1)
    def _():
        z_copy(z, 0).start()

    @pl.when(z > 0)
    def _():
        z_copy(z, 1).start()

    spread(z)

    for h in range(HEADS):
        cols = slice(h * HD, (h + 1) * HD)
        vt[h, 0:HD, :] = win_ref[1, :, cols].astype(F32).T.astype(BF)
        vt[h, HD : HD + 16, :] = jnp.ones((16, CACHE), BF)
        va[h, 0:HD, :] = local_ref[2, :, cols].astype(F32).T.astype(BF)
        va[h, HD : HD + 16, :] = jnp.ones((16, ROWS), BF)
    lpart[...] = jnp.zeros_like(lpart)

    @pl.when(z == 0)
    def _():
        zo_recv[0] = jnp.zeros((NZ, SHARE, HD), BF)
        zl_recv[0] = jnp.full((NZ, 8, HD), NONE, F32)

    @pl.when(z == NZ - 1)
    def _():
        zo_recv[1] = jnp.zeros((NZ, SHARE, HD), BF)
        zl_recv[1] = jnp.full((NZ, 8, HD), NONE, F32)

    def attend(column, half):
        def head(h, carry):
            cols = pl.ds(pl.multiple_of(h * HD, HD), HD)
            q = qbuf[column, pl.ds(4 * half, 4), :, cols].reshape(PACK, HD)
            nt = (((1,), (1,)), ((), ()))
            sc = lax.dot_general(win_ref[0, :, cols], q, nt, preferred_element_type=F32)
            sa = lax.dot_general(local_ref[1, :, cols], q, nt, preferred_element_type=F32)
            bias = bias_ref[pl.ds(h, 1), :]
            top = jnp.maximum(
                jnp.max(sc, axis=0, keepdims=True) * COEF - bias,
                jnp.max(sa, axis=0, keepdims=True) * COEF,
            )
            pc = jnp.exp2(sc * COEF - (top + bias)).astype(BF)
            pa = jnp.exp2(sa * COEF - top).astype(BF)
            acc = jnp.dot(vt[h], pc, preferred_element_type=F32) + jnp.dot(
                va[h], pa, preferred_element_type=F32
            )
            total = acc[HD : HD + 1]
            opart[column * 2 + half, cols, :] = (acc[:HD] * (1.0 / total)).astype(BF)
            lpart[column, pl.ds(half * 4 + h, 1), :] = top + jnp.log2(total)
            return carry

        lax.fori_loop(0, HEADS, head, 0)

    def arrivals(which, half):
        @pl.when(which == 1)
        def _():
            for j in (0, 2):
                y_wait(4 * half + j, 1)

        @pl.when(which == 2)
        def _():
            for j in (1, 3):
                y_wait(4 * half + j, 0)

        @pl.when(which == 3)
        def _():
            for j in range(4):
                y2_wait(4 * half + j)

    def pass_on(block):
        odd = block % 2

        @pl.when(odd == 0)
        def _():
            y_wait(block, 0)

        @pl.when(odd == 1)
        def _():
            y_wait(block, 1)

        y2_copy(block, odd).start()

    def gather_step(t, carry):
        @pl.when(jnp.logical_and(t >= 1, t < NZ))
        def _():
            @pl.when(z - t >= 0)
            def _():
                z_wait(z - t)

                @pl.when(z < NZ - 1)
                def _():
                    z_copy(z - t, 0).start()

                spread(z - t)

            @pl.when(z + t < NZ)
            def _():
                z_wait(z + t)

                @pl.when(z > 0)
                def _():
                    z_copy(z + t, 1).start()

                spread(z + t)

        @pl.when(jnp.logical_and(t >= 1, t <= NZ))
        def _():
            @pl.when(z - (t - 1) >= 0)
            def _():
                pass_on(z - (t - 1))

            @pl.when(jnp.logical_and(t > 1, z + (t - 1) < NZ))
            def _():
                pass_on(z + (t - 1))

        @pl.when(t == NZ)
        def _():
            for half in range(2):
                @pl.when(z // 2 + 4 * half != z)
                def _():
                    evict_z(half).start()

            @pl.when(jnp.logical_or(z == 0, z == NZ - 1))
            def _():
                evict_own().start()

        @pl.when(t >= 4)
        def _():
            b = t - 4
            half = jnp.where(b < 4, near, far)
            which = b % 4
            column = (y + which + jnp.where(which == 2, 1, 0) - jnp.where(which == 3, 1, 0)) % NY
            arrivals(which, half)
            attend(column, half)

        return carry

    lax.fori_loop(0, NZ + 4, gather_step, 0)

    def lse_copy(i):
        src, dev = ((yp, yp), (ym, ym), (y2, y2), (y2, yp), (y2, ym))[i]
        return copy(lpart.at[src], lrecv.at[i], ls_sem.at[i], lr_sem.at[i], at(z, dev))

    for i in range(5):
        lse_copy(i).start()

    def unit(u):
        half = jnp.where(u < 3, far, near)
        h = u % 3
        odd = u % 2
        cols = pl.ds(pl.multiple_of(h * HD, HD), HD)
        return half, h, odd, cols

    def raw1(u):
        half, h, odd, cols = unit(u)
        return copy(
            opart.at[y2 * 2 + half, cols, :], r1.at[u], r1s.at[u], r1r.at[u],
            at(z, yp + odd * (ym - yp)),
        )

    def raw2(u):
        half, h, odd, cols = unit(u)
        column = ym + odd * (yp - ym)
        return copy(
            opart.at[column * 2 + half, cols, :], r2.at[u], r2s.at[u], r2r.at[u], at(z, column)
        )

    def fwd(u):
        odd = u % 2
        return copy(
            relayed.at[u], r3.at[u], r3s.at[u], r3r.at[u], at(z, yp + odd * (ym - yp))
        )

    for u in range(2):
        raw1(u).start()
        raw2(u).start()

    for i in range(5):
        lse_copy(i).wait_recv()
    for side, column in ((0, yp), (1, ym)):
        got, own = lrecv[3 + side], lpart[column]
        both = lse2(got, own)
        wrelay[side, 0] = jnp.exp2(got - both)
        wrelay[side, 1] = jnp.exp2(own - both)
    own = lpart[y]
    everything = lse2(lrecv[0], lrecv[1], lrecv[2], own)
    w_m, w_p, w_2 = (jnp.exp2(lrecv[i] - everything) for i in range(3))
    wfinal[0, 0] = jnp.exp2(own - everything)
    wfinal[0, 1] = w_m + w_2
    wfinal[0, 2] = w_p
    wfinal[1, 0] = jnp.exp2(own - everything)
    wfinal[1, 1] = w_p + w_2
    wfinal[1, 2] = w_m
    for j in range(4):
        shifted = everything if j == 0 else pltpu.roll(everything, PACK - ROWS * j, 1)
        zl_own[j] = shifted[:, :HD]

    def relay(u):
        half, h, odd, cols = unit(u)
        row = pl.ds(half * 4 + h, 1)
        raw1(u).wait_recv()
        column = yp + odd * (ym - yp)
        mixed = r1[u].astype(F32) * wrelay[odd, 0, row, :] + opart[
            column * 2 + half, cols, :
        ].astype(F32) * wrelay[odd, 1, row, :]
        relayed[u] = mixed.astype(BF)
        fwd(u).start()

    def final(u):
        half, h, odd, cols = unit(u)
        row = pl.ds(half * 4 + h, 1)
        raw2(u).wait_recv()
        fwd(u).wait_recv()
        mixed = (
            opart[y * 2 + half, cols, :].astype(F32) * wfinal[odd, 0, row, :]
            + r3[u].astype(F32) * wfinal[odd, 1, row, :]
            + r2[u].astype(F32) * wfinal[odd, 2, row, :]
        )
        for j in range(4):
            shifted = mixed if j == 0 else pltpu.roll(mixed, PACK - ROWS * j, 1)
            zo_own[4 * half + j, cols, :] = shifted[:, :HD]

    def zo_copy(block, h, side):
        cols = pl.ds(pl.multiple_of(h * HD, HD), HD)
        return copy(
            zo_out.at[block, cols, :], zo_recv.at[side, block, cols, :], zos.at[block, h],
            zor.at[side, block, h], at(z + 1 - 2 * side, y),
        )

    def zl_copy(block, side):
        return copy(
            zl_out.at[block], zl_recv.at[side, block], zls.at[block], zlr.at[side, block],
            at(z + 1 - 2 * side, y),
        )

    def zo_wait(block, h, side):
        cols = pl.ds(pl.multiple_of(h * HD, HD), HD)
        copy(
            zo_out.at[block, cols, :], zo_recv.at[side, block, cols, :], zos.at[block, h],
            zor.at[side, block, h], at(z, yp),
        ).wait_recv()

    def zl_wait(block, side):
        copy(
            zl_out.at[block], zl_recv.at[side, block], zls.at[block], zlr.at[side, block],
            at(z, yp),
        ).wait_recv()

    def along(block, j, half, h, side):
        inner = z > 0 if side == 0 else z < NZ - 1

        @pl.when(h == 0)
        def _():
            @pl.when(inner)
            def _():
                zl_wait(block, side)

            got, own = zl_recv[side, block], zl_own[j]
            both = lse2(got, own)
            zl_out[block] = both
            zl_copy(block, side).start()
            wz[block, 0] = jnp.exp2(got - both)
            wz[block, 1] = jnp.exp2(own - both)

        @pl.when(inner)
        def _():
            zo_wait(block, h, side)

        cols = pl.ds(pl.multiple_of(h * HD, HD), HD)
        row = pl.ds(half * 4 + h, 1)
        mixed = (
            zo_recv[side, block, cols, :].astype(F32) * wz[block, 0, row, :]
            + zo_own[block, cols, :] * wz[block, 1, row, :]
        )
        zo_out[block, cols, :] = mixed.astype(BF)
        zo_copy(block, h, side).start()

    def z_phase(half, h):
        for j in (3, 0, 2, 1):
            block = 4 * half + j

            @pl.when(block > z)
            def _():
                along(block, j, half, h, 0)

            @pl.when(block < z)
            def _():
                along(block, j, half, h, 1)

    place = z + near * (NZ - 1 - 2 * z)

    def reduce_step(u, carry):
        @pl.when(u + 2 < 6)
        def _():
            raw1(u + 2).start()
            raw2(u + 2).start()

        @pl.when(u < 6)
        def _():
            relay(u)

        @pl.when(jnp.logical_and(u >= 1, u <= 6))
        def _():
            final(u - 1)

        uz = u - 1 - place

        @pl.when(jnp.logical_and(uz >= 0, uz < 3))
        def _():
            z_phase(far, uz)

        @pl.when(u == 5)
        def _():
            for which in range(2):
                @pl.when(2 * (z % 4) + which != z)
                def _():
                    rows = evict_rows(which, y)
                    copy(rows, rows, ezs.at[0], ezr.at[which], at(z, yp)).wait_recv()

            @pl.when(jnp.logical_or(z == 0, z == NZ - 1))
            def _():
                evict_own().wait()

            for which in range(2):
                evict_y(which, 0).start()
                evict_y(which, 1).start()

        @pl.when(u >= 5)
        def _():
            z_phase(near, u - 5)

        return carry

    lax.fori_loop(0, 8, reduce_step, 0)

    evict_y_wait(0, 0)
    evict_y2(0).start()
    evict_y_wait(1, 1)
    evict_y2(1).start()

    j = z % 4

    @pl.when(z > 0)
    def _():
        zl_wait(z, 0)

    @pl.when(z < NZ - 1)
    def _():
        zl_wait(z, 1)

    first, second, own = zl_recv[0, z], zl_recv[1, z], zl_own[j]
    total = lse2(first, second, own)
    wz[z, 0] = jnp.exp2(first - total)
    wz[z, 1] = jnp.exp2(second - total)
    wz[z, 2] = jnp.exp2(own - total)
    for h in range(HEADS):
        cols = pl.ds(h * HD, HD)
        row = pl.ds(near * 4 + h, 1)

        @pl.when(z > 0)
        def _():
            zo_wait(z, h, 0)

        @pl.when(z < NZ - 1)
        def _():
            zo_wait(z, h, 1)

        mixed = (
            zo_recv[0, z, cols, :].astype(F32) * wz[z, 0, row, :]
            + zo_recv[1, z, cols, :].astype(F32) * wz[z, 1, row, :]
            + zo_own[z, cols, :] * wz[z, 2, row, :]
        )
        out_ref[:, h * HD : (h + 1) * HD] = mixed.T[:ROWS].astype(BF)

    evict_y_wait(1, 0)
    evict_y_wait(0, 1)
    evict_y2_wait(0)
    evict_y2_wait(1)

    def drain(block, carry):
        @pl.when(jnp.logical_and(block <= z, z < NZ - 1))
        def _():
            z_copy(block, 0).wait_send()

        @pl.when(jnp.logical_and(block >= z, z > 0))
        def _():
            z_copy(block, 1).wait_send()

        y_copy(block, 0).wait_send()
        y_copy(block, 1).wait_send()
        y2_copy(block, block % 2).wait_send()

        @pl.when(block != z)
        def _():
            side = jnp.where(block > z, 0, 1)
            zl_copy(block, side).wait_send()
            for h in range(HEADS):
                zo_copy(block, h, side).wait_send()

        return carry

    lax.fori_loop(0, NZ, drain, 0)

    def drain_units(u, carry):
        raw1(u).wait_send()
        raw2(u).wait_send()
        fwd(u).wait_send()
        return carry

    lax.fori_loop(0, 6, drain_units, 0)
    for i in range(5):
        lse_copy(i).wait_send()
    for half in range(2):
        @pl.when(z // 2 + 4 * half != z)
        def _():
            evict_z(half).wait_send()
    for which in range(2):
        evict_y(which, 0).wait_send()
        evict_y(which, 1).wait_send()
        evict_y2(which).wait_send()


def attention(local, window, bias):
    dma = pltpu.SemaphoreType.DMA
    vm = pltpu.VMEM
    return pl.pallas_call(
        kernel,
        out_shape=(
            jax.ShapeDtypeStruct((ROWS, SHARE), BF),
            jax.ShapeDtypeStruct((2, CACHE, SHARE), BF),
        ),
        in_specs=[pl.BlockSpec(memory_space=pltpu.VMEM)] * 3,
        out_specs=(
            pl.BlockSpec(memory_space=pltpu.VMEM),
            pl.BlockSpec(memory_space=pl.ANY),
        ),
        scratch_shapes=[
            vm((NY, NZ, ROWS, SHARE), BF),
            vm((HEADS, HD + 16, CACHE), BF),
            vm((HEADS, HD + 16, ROWS), BF),
            vm((2 * NY, SHARE, PACK), BF),
            vm((NY, 8, PACK), F32),
            vm((5, 8, PACK), F32),
            vm((2, 2, 8, PACK), F32),
            vm((2, 3, 8, PACK), F32),
            vm((4, 8, HD), F32),
            vm((6, HD, PACK), BF),
            vm((6, HD, PACK), BF),
            vm((6, HD, PACK), BF),
            vm((6, HD, PACK), BF),
            vm((NZ, SHARE, HD), F32),
            vm((2, NZ, SHARE, HD), BF),
            vm((NZ, SHARE, HD), BF),
            vm((2, NZ, 8, HD), F32),
            vm((NZ, 8, HD), F32),
            vm((NZ, 3, 8, HD), F32),
            dma((2, NZ)), dma((NZ,)), dma((2, NZ)), dma((2, NZ)), dma((NZ,)), dma((NZ,)),
            dma((5,)), dma((5,)), dma((6,)), dma((6,)), dma((6,)), dma((6,)), dma((6,)), dma((6,)),
            dma((NZ, HEADS)), dma((2, NZ, HEADS)), dma((NZ,)), dma((2, NZ)),
            dma((2,)), dma((2,)), dma((2, 2)), dma((2, 2)), dma((2,)), dma((2,)), dma(()),
        ],
        compiler_params=pltpu.CompilerParams(
            collective_id=0, has_side_effects=True, vmem_limit_bytes=48 * 1024 * 1024
        ),
        cost_estimate=pl.CostEstimate(
            flops=4 * 3072 * 864 * SHARE, bytes_accessed=4 * 2**20, transcendentals=3072 * 864 * 3
        ),
    )(local, window, bias)


def body(active_qkv, window_kv, slot_owner, oldest_slot, timestep, time_slopes, gate_table):
    tok_dev = active_qkv.shape[1]
    ways = lax.axis_size("sp")
    groups = lax.axis_size("grp")
    split = active_qkv.reshape(3, tok_dev, ways, SHARE)
    local = lax.all_to_all(split, "sp", split_axis=2, concat_axis=1, tiled=True).reshape(
        3, ROWS, SHARE
    )
    group = lax.axis_index("grp")
    oldest = oldest_slot[0]
    group_ids = jnp.arange(groups, dtype=jnp.int32)
    my_slot = jnp.sum(jnp.where(group_ids == group, slot_owner, 0))
    age = (WIN - jnp.mod(my_slot - oldest, WIN)).astype(F32)
    slopes = lax.dynamic_slice_in_dim(time_slopes, lax.axis_index("sp") * HEADS, HEADS)
    bias = jnp.pad(slopes * (age * LOG2E), (0, 8 - HEADS))
    combined, moved = attention(local, window_kv, jnp.broadcast_to(bias[:, None], (8, PACK)))
    new_window = jnp.where(my_slot == oldest, moved, window_kv)
    returned = lax.all_to_all(combined, "sp", split_axis=0, concat_axis=1, tiled=True)
    gate = lax.dynamic_slice_in_dim(gate_table, timestep[0], 1, 0)
    attended = (gate * returned.astype(F32)).astype(BF)
    return (attended, new_window)


def solution(mesh):
    in_specs = (P(None, ("grp", "sp"), None), P(None, "grp", "sp"), P(), P(), P(), P(), P())
    out_specs = (P(("grp", "sp"), None), P(None, "grp", "sp"))
    return jax.shard_map(body, mesh=mesh, in_specs=in_specs, out_specs=out_specs, check_vma=False)
```

time: 663 us -> 167 us (0.25)
  the two profiles are of different devices: /device:TPU:6 before, /device:TPU:1 now
where the time goes in v1:
time: 167 us; the launch traced here: 166 us
  Pallas kernels  93.9 us (56%)
  starting transfers between devices  35.3 us (21%)
  waiting for transfers between devices  27.2 us (16%)
  local copies, waits for them, and re-layouts  4.02 us (2%)
  between operations  3.34 us (2%)
  other arithmetic  2.54 us (2%)
    pallas_call x1, Pallas kernels, attention(): pl.pallas_call(kernel, out_shape=(jax.ShapeDtypeStruct((ROWS, SHARE), BF)...  93.9 us
    all_to_all x1, starting transfers between devices, body(): lax.all_to_all(split, 'sp', split_axis=2, concat_axis=1, tiled=True)  19.1 us
    all_to_all x1, starting transfers between devices, body(): lax.all_to_all(combined, 'sp', split_axis=0, concat_axis=1, tiled=True)  16.3 us
    all_to_all x1, waiting for transfers between devices, body(): lax.all_to_all(combined, 'sp', split_axis=0, concat_axis=1, tiled=True)  13.8 us
    all_to_all x1, waiting for transfers between devices, body(): lax.all_to_all(split, 'sp', split_axis=2, concat_axis=1, tiled=True)  13.4 us
  transfers between devices with their start and end apart: 2, of which 2 were waited for; matrix products, arithmetic and copies ran while one was open for 1% of the time, Pallas kernels for 0%

profile of v1, /device:TPU:1, one launch (start us, length us, event | category | flops | bytes accessed | tf_op | source)
XLA Modules:
  0.0 166.3 jit_solution(11584167191351041214)
XLA Ops:
  0.6 0.0 copy-start
  0.6 0.0 copy-start.4
  0.7 0.0 copy-start.3
  0.7 1.3 reshape.17
  2.0 0.0 copy-start.1
  2.0 0.8 copy.12
  2.8 19.1 %all-to-all-start = ((bf16[3,6,16,384]{3,1,0,2:T(8,128)(2,1)}), bf16[3,6,16,384]{3,1,0,2:T(8,128)(2,1)S(1)}, u32[]{:S(2)}, u32[]{:S(2)}) async-start(bf16[3,6,16,384]{3,1,0,2:T(8,128)(2,1)} %copy.12), calls=%async_computation | async-start | bytes 589824 | tf_op jit(solution)/shard_map/all_to_all | solution.py:616
  21.9 0.0 copy-done.4
  21.9 0.6 fusion
  25.1 0.0 copy-done.3
  25.1 0.1 dynamic-slice_multiply_fusion
  25.2 0.0 copy-done
  25.2 13.4 %all-to-all-done = bf16[3,6,16,384]{3,1,0,2:T(8,128)(2,1)S(1)} async-done(((bf16[3,6,16,384]{3,1,0,2:T(8,128)(2,1)}), bf16[3,6,16,384]{3,1,0,2:T(8,128)(2,1)S(1)}, u32[]{:S(2)}, u32[]{:S(2)}) %all-to-all-start) | async-done | bytes 221216 | tf_op jit(solution)/shard_map/all_to_all | solution.py:616
  38.7 0.1 reshape.18.local_ref
  38.8 0.1 broadcast_in_dim.11.bias_ref
  38.8 0.0 copy-done.1
  38.8 93.9 %shard_map.86 = (bf16[96,384]{1,0:T(8,128)(2,1)S(1)}, bf16[2,768,384]{2,1,0:T(8,128)(2,1)S(1)}) custom-call(bf16[3,96,384]{2,1,0:T(8,128)(2,1)S(1)} %reshape.18.local_ref, bf16[2,768,384]{2,1,0:T(8,128)(2,1)S(1)} %copy-done.1, f32[8,384]{1,0:T(8,128)S(1)} %broadcast_in_dim.11.bias_ref), custom_call_target="tpu_custom_call" | custom-call | flops 4076863488 | bytes 4194304 | tf_op jit(solution)/shard_map/pallas_call | solution.py:566
  132.7 0.0 copy-start.2
  132.8 1.0 copy-done.2
  133.8 0.7 all_to_all.24
  134.4 16.3 %all-to-all-start.1 = ((bf16[16,6,384]{2,1,0:T(8,128)(2,1)}), bf16[16,6,384]{2,1,0:T(8,128)(2,1)S(1)}, u32[]{:S(2)}, u32[]{:S(2)}) async-start(bf16[16,6,384]{2,1,0:T(8,128)(2,1)} %all_to_all.24), calls=%async_computation.1 | async-start | bytes 196608 | tf_op jit(solution)/shard_map/all_to_all | solution.py:628
  150.7 1.2 broadcast_select_fusion
  151.9 13.8 %all-to-all-done.1 = bf16[16,6,384]{2,1,0:T(8,128)(2,1)S(1)} async-done(((bf16[16,6,384]{2,1,0:T(8,128)(2,1)}), bf16[16,6,384]{2,1,0:T(8,128)(2,1)S(1)}, u32[]{:S(2)}, u32[]{:S(2)}) %all-to-all-start.1) | async-done | bytes 73760 | tf_op jit(solution)/shard_map/all_to_all | solution.py:628
  165.6 0.7 multiply_convert_fusion
  (4 shorter events, 0.1 us)
Async XLA Ops:
  0.6 24.6 %copy-start = (f32[50,6144]{1,0:T(8,128)S(1)}, f32[50,6144]{1,0:T(8,128)}, u32[]{:S(2)}) copy-start(f32[50,6144]{1,0:T(8,128)} %param.13) | copy-start | bytes 3686404
  0.6 21.2 %copy-start.4 = (s32[32]{0:T(128)S(1)}, s32[32]{0:T(128)}, u32[]{:S(2)}) copy-start(s32[32]{0:T(128)} %param.9) | copy-start | bytes 388
  0.7 24.5 %copy-start.3 = (f32[48]{0:T(128)S(1)}, f32[48]{0:T(128)}, u32[]{:S(2)}) copy-start(f32[48]{0:T(128)} %param.12) | copy-start | bytes 580
  2.0 36.8 %copy-start.1 = (bf16[2,768,384]{2,1,0:T(8,128)(2,1)S(1)}, bf16[2,768,384]{2,1,0:T(8,128)(2,1)}, u32[]{:S(2)}) copy-start(bf16[2,768,384]{2,1,0:T(8,128)(2,1)} %win_ref.1) | copy-start | bytes 3538948
  2.8 35.8 %all-to-all-start = ((bf16[3,6,16,384]{3,1,0,2:T(8,128)(2,1)}), bf16[3,6,16,384]{3,1,0,2:T(8,128)(2,1)S(1)}, u32[]{:S(2)}, u32[]{:S(2)}) async-start(bf16[3,6,16,384]{3,1,0,2:T(8,128)(2,1)} %copy.12), calls=%async_computation | async-start | bytes 589824 | tf_op jit(solution)/shard_map/all_to_all | solution.py:616
  132.7 1.0 copy-start.2
  134.4 31.2 %all-to-all-start.1 = ((bf16[16,6,384]{2,1,0:T(8,128)(2,1)}), bf16[16,6,384]{2,1,0:T(8,128)(2,1)S(1)}, u32[]{:S(2)}, u32[]{:S(2)}) async-start(bf16[16,6,384]{2,1,0:T(8,128)(2,1)} %all_to_all.24), calls=%async_computation.1 | async-start | bytes 196608 | tf_op jit(solution)/shard_map/all_to_all | solution.py:628

commit v2 on v0

v2 whole, which is shorter than its diff:
```python
import functools
import math

import jax
import jax.numpy as jnp
from jax import lax
from jax.experimental import pallas as pl
from jax.experimental.pallas import tpu as pltpu
from jax.sharding import PartitionSpec as P

HD = 128
WIN = 8
HEADS = 3
SHARE = HEADS * HD
TOK = 6
ROWS = 96
HALF = 48
CACHE = 768
NZ = 8
NY = 4
NXC = 8
PACK = 4 * ROWS
OUT1 = 112
BACK1 = 48
SUMS = HD + 16
LOG2E = math.log2(math.e)
COEF = LOG2E / math.sqrt(HD)
NONE = -1e30
MESH = pl.DeviceIdType.MESH
BF = jnp.bfloat16
F32 = jnp.float32
NT = (((1,), (1,)), ((), ()))


def lse2(*parts):
    top = functools.reduce(jnp.maximum, parts)
    return top + jnp.log2(sum(jnp.exp2(p - top) for p in parts))


def kernel(
    x_ref, win_ref, owner_ref, oldest_ref, slope_ref, out_ref, moved_ref,
    pack32, packb, recv1, dense, local, qbuf, kbuf, vt, akv, vta, acc_ref,
    zo_own, zo_recv, zo_out, zl_own, zl_recv, zl_out, comb, back, ret, recv2,
    s1s, s1r, s2s, s2r, zsend, zrecv, ks, kr, vs, vr, acs, acr,
    zos, zor, zls, zlr, ezs, ezr, eys, eyr, cs, cr, ds, dr, cp_sem,
):
    me = lax.axis_index("grp")
    sp = lax.axis_index("sp")
    z = me // NY
    y = me % NY
    zh = sp // NXC
    xc = sp % NXC
    near = z // 4
    far = 1 - near

    def at(zz, yy):
        return {"grp": zz * NY + yy, "sp": sp}

    def beside(other):
        return {"grp": me, "sp": zh * NXC + other}

    across = {"grp": me, "sp": (1 - zh) * NXC + xc}

    def copy(src, dst, send, recv, dev):
        return pltpu.make_async_remote_copy(
            src_ref=src, dst_ref=dst, send_sem=send, recv_sem=recv,
            device_id=dev, device_id_type=MESH,
        )

    def head_cols(h):
        return pl.ds(pl.multiple_of(h * HD, HD), HD)

    barrier = pltpu.get_barrier_semaphore()
    peers = [at((z + i) % NZ, y) for i in range(1, NZ)]
    peers += [at(z, (y + i) % NY) for i in range(1, NY)]
    peers += [beside((xc + i) % NXC) for i in range(1, NXC)]
    peers += [across]
    for peer in peers:
        pl.semaphore_signal(barrier, inc=1, device_id=peer, device_id_type=MESH)
    pl.semaphore_wait(barrier, len(peers))

    def k_copy(h, i):
        return copy(
            win_ref.at[0, :, h * HD : (h + 1) * HD], kbuf.at[y, h], ks.at[i, h], kr.at[i, h],
            at(z, (y + i) % NY),
        )

    def v_copy(h, i):
        return copy(
            vt.at[y, h, pl.ds(0, HD), :], vt.at[y, h, pl.ds(0, HD), :], vs.at[i, h], vr.at[i, h],
            at(z, (y + i) % NY),
        )

    def kv_wait(h, i):
        src = (y + NY - i) % NY
        copy(kbuf.at[src, h], kbuf.at[src, h], ks.at[i, h], kr.at[i, h], at(z, src)).wait_recv()
        rows = vt.at[src, h, pl.ds(0, HD), :]
        copy(rows, rows, vs.at[i, h], vr.at[i, h], at(z, src)).wait_recv()

    for i in (1, 3, 2):
        k_copy(0, i).start()

    def step1(other):
        return copy(packb.at[other], recv1.at[xc], s1s.at[other], s1r.at[xc], beside(other))

    def step1_wait(other):
        copy(recv1.at[other], recv1.at[other], s1s.at[other], s1r.at[other], beside(other)).wait_recv()

    def piece(half, t, h):
        return half * 54 + (t * HEADS + h) * TOK

    for d in range(NXC):
        for half in range(2):
            for t in range(3):
                for h in range(HEADS):
                    col = ((half * NXC + d) * HEADS + h) * HD
                    row = piece(half, t, h)
                    pack32[d, row : row + TOK, :] = x_ref[t, :, col : col + HD].astype(F32)
        packb[d] = pack32[d].astype(BF)
    for i in range(1, NXC):
        step1((xc + i) % NXC).start()
    recv1[xc] = packb[xc]

    for h in range(HEADS):
        vt[y, h, 0:HD, :] = win_ref[1, :, h * HD : (h + 1) * HD].astype(F32).T.astype(BF)
        if h < 2:
            for i in (1, 3, 2):
                v_copy(h, i).start()
        if h == 0:
            for i in (1, 3, 2):
                k_copy(1, i).start()
        kbuf[y, h] = win_ref[0, :, h * HD : (h + 1) * HD]
        for src in range(NY):
            vt[src, h, HD:SUMS, :] = jnp.ones((SUMS - HD, CACHE), BF)
        vta[h, HD:SUMS, :] = jnp.ones((SUMS - HD, PACK), BF)

    @pl.when(z == 0)
    def _():
        zo_recv[0] = jnp.zeros((NZ, SHARE, HD), BF)
        zl_recv[0] = jnp.full((NZ, HEADS, 8, HD), NONE, F32)

    @pl.when(z == NZ - 1)
    def _():
        zo_recv[1] = jnp.zeros((NZ, SHARE, HD), BF)
        zl_recv[1] = jnp.full((NZ, HEADS, 8, HD), NONE, F32)

    for i in range(1, NXC):
        step1_wait((xc + i) % NXC)
    for s in range(NXC):
        pack32[s] = recv1[s].astype(F32)
    for t in range(3):
        for s in range(NXC):
            for half in range(2):
                for h in range(HEADS):
                    row = piece(half, t, h)
                    dense[half, t, s * TOK : (s + 1) * TOK, h * HD : (h + 1) * HD] = pack32[
                        s, row : row + TOK, :
                    ]

    mine = pl.ds(pl.multiple_of(zh * HALF, HALF), HALF)
    theirs = pl.ds(pl.multiple_of((1 - zh) * HALF, HALF), HALF)

    def step2(t, n):
        part = back.at[pl.ds(t, n)]
        return copy(part, local.at[pl.ds(t, n), mine, :], s2s.at[t], s2r.at[t], across)

    def step2_wait(t, n):
        part = local.at[pl.ds(t, n), theirs, :]
        copy(part, part, s2s.at[t], s2r.at[t], across).wait_recv()

    back[0] = dense[1 - zh, 0].astype(BF)
    step2(0, 1).start()
    for t in (1, 2):
        back[t] = dense[1 - zh, t].astype(BF)
    step2(1, 2).start()
    for t in range(3):
        local[t, mine, :] = dense[zh, t].astype(BF)

    def z_copy(block, h, side):
        part = qbuf.at[block, :, head_cols(h)]
        return copy(
            part, part, zsend.at[side, block, h], zrecv.at[block, h], at(z + 1 - 2 * side, y)
        )

    def z_wait(block, h):
        part = qbuf.at[block, :, head_cols(h)]
        copy(part, part, zsend.at[0, block, h], zrecv.at[block, h], across).wait_recv()

    step2_wait(0, 1)
    qbuf[z] = local[0]
    for h in range(HEADS):
        @pl.when(z < NZ - 1)
        def _():
            z_copy(z, h, 0).start()

        @pl.when(z > 0)
        def _():
            z_copy(z, h, 1).start()

    def gather_step(t):
        for h in range(HEADS):
            @pl.when(z - t >= 0)
            def _():
                z_wait(z - t, h)

                @pl.when(z < NZ - 1)
                def _():
                    z_copy(z - t, h, 0).start()

            @pl.when(z + t < NZ)
            def _():
                z_wait(z + t, h)

                @pl.when(z > 0)
                def _():
                    z_copy(z + t, h, 1).start()

    def a_copy(i):
        return copy(akv.at[y], akv.at[y], acs.at[i], acr.at[i], at(z, (y + i) % NY))

    def a_wait(i):
        src = (y + NY - i) % NY
        copy(akv.at[src], akv.at[src], acs.at[i], acr.at[i], at(z, src)).wait_recv()

    def evict_rows(which, column):
        return moved_ref.at[:, pl.ds((which * NY + column) * ROWS, ROWS), :]

    def evict_z(half):
        return copy(
            akv.at[y], evict_rows(z % 2, y), ezs.at[half], ezr.at[z % 2], at(z // 2 + 4 * half, y)
        )

    def evict_own():
        return pltpu.make_async_copy(akv.at[y], evict_rows(z % 2, y), cp_sem)

    def evict_y(which, i):
        rows = evict_rows(which, y)
        return copy(rows, rows, eys.at[which, i], eyr.at[which, i], at(z, (y + i) % NY))

    def evict_y_wait(which, i):
        src = (y + NY - i) % NY
        rows = evict_rows(which, src)
        copy(rows, rows, eys.at[which, i], eyr.at[which, i], at(z, src)).wait_recv()

    def attend(h, half):
        cols = head_cols(h)
        q = qbuf[pl.ds(4 * half, 4), :, cols].reshape(PACK, HD)
        slope = slope_ref[sp * HEADS + h] * LOG2E

        sa = lax.dot_general(
            akv[:, 0, :, cols].reshape(PACK, HD), q, NT, preferred_element_type=F32
        )
        first = jnp.max(sa, axis=0, keepdims=True) * COEF
        pa = jnp.exp2(sa * COEF - first).astype(BF)
        acc_ref[...] = jnp.dot(vta[h], pa, preferred_element_type=F32)

        def chunk(src, top):
            slot = owner_ref[z * NY + src] - oldest_ref[0]
            age = WIN - (slot + WIN) % WIN
            bias = slope * age.astype(F32)
            s = lax.dot_general(kbuf[src, h], q, NT, preferred_element_type=F32)
            new = jnp.maximum(top, jnp.max(s, axis=0, keepdims=True) * COEF - bias)
            p = jnp.exp2(s * COEF - (new + bias)).astype(BF)
            acc_ref[...] = acc_ref[...] * jnp.exp2(top - new) + jnp.dot(
                vt[src, h], p, preferred_element_type=F32
            )
            return new

        top = lax.fori_loop(0, NY, chunk, first)
        total = acc_ref[HD : HD + 1, :]
        mixed = acc_ref[0:HD, :] * (1.0 / total)
        lse = jnp.broadcast_to(top + jnp.log2(total), (8, PACK))
        for j in range(4):
            back_by = PACK - ROWS * j
            part = mixed if j == 0 else pltpu.roll(mixed, back_by, 1)
            zo_own[4 * half + j, cols, :] = part[:, :HD]
            part = lse if j == 0 else pltpu.roll(lse, back_by, 1)
            zl_own[4 * half + j, h] = part[:, :HD]

    def zo_copy(block, h, side, dev):
        cols = head_cols(h)
        return copy(
            zo_out.at[block, cols, :], zo_recv.at[side, block, cols, :], zos.at[block, h],
            zor.at[side, block, h], dev,
        )

    def zl_copy(block, h, side, dev):
        return copy(
            zl_out.at[block, h], zl_recv.at[side, block, h], zls.at[block, h],
            zlr.at[side, block, h], dev,
        )

    def along(block, h, side):
        inner = z > 0 if side == 0 else z < NZ - 1
        onward = at(z + 1 - 2 * side, y)
        cols = head_cols(h)

        @pl.when(inner)
        def _():
            zl_copy(block, h, side, across).wait_recv()
            zo_copy(block, h, side, across).wait_recv()

        got, own = zl_recv[side, block, h], zl_own[block, h]
        both = lse2(got, own)
        zl_out[block, h] = both
        mixed = (
            zo_recv[side, block, cols, :].astype(F32) * jnp.exp2(got - both)[0:1]
            + zo_own[block, cols, :] * jnp.exp2(own - both)[0:1]
        )
        zo_out[block, cols, :] = mixed.astype(BF)
        zl_copy(block, h, side, onward).start()
        zo_copy(block, h, side, onward).start()

    def upward(h, half):
        for j in (3, 2, 1, 0):
            @pl.when(4 * half + j > z)
            def _():
                along(4 * half + j, h, 0)

    def downward(h, half):
        for j in range(4):
            @pl.when(4 * half + j < z)
            def _():
                along(4 * half + j, h, 1)

    def tick(e, carry):
        @pl.when(e < NZ)
        def _():
            gather_step(e)

        @pl.when(e == 2)
        def _():
            step2_wait(1, 2)
            akv[y] = local[1:3]
            for i in (1, 3, 2):
                a_copy(i).start()
            for i in (1, 3, 2):
                k_copy(2, i).start()
                v_copy(2, i).start()

        @pl.when(e == NZ - 1)
        def _():
            for half in range(2):
                @pl.when(z // 2 + 4 * half != z)
                def _():
                    evict_z(half).start()

            @pl.when(jnp.logical_or(z == 0, z == NZ - 1))
            def _():
                evict_own().start()

        @pl.when(e == 6)
        def _():
            for i in (1, 3, 2):
                a_wait(i)
            for h in range(HEADS):
                values = akv[:, 1, :, h * HD : (h + 1) * HD].reshape(PACK, HD)
                vta[h, 0:HD, :] = values.astype(F32).T.astype(BF)

        for h, first in ((0, 6), (1, 9), (2, 11)):
            @pl.when(e == first)
            def _():
                for i in (1, 3, 2):
                    kv_wait(h, i)

        @pl.when(jnp.logical_or(e == 6, jnp.logical_and(e >= 8, e <= 12)))
        def _():
            h = jnp.where(e >= 11, 2, jnp.where(e >= 9, 1, 0))
            is_near = jnp.logical_or(e == 6, jnp.logical_or(e == 10, e == 12))
            attend(h, jnp.where(is_near, near, far))

        def sums(h, carry):
            far_at = 8 + h + h // 2
            near_at = 8 + 2 * h

            @pl.when(e == far_at + z)
            def _():
                upward(h, 1)

            @pl.when(e == far_at + NZ - 1 - z)
            def _():
                downward(h, 0)

            @pl.when(jnp.logical_and(z < 3, e == near_at + z))
            def _():
                upward(h, 0)

            @pl.when(jnp.logical_and(z > 4, e == near_at + NZ - 1 - z))
            def _():
                downward(h, 1)

            return carry

        @pl.when(e >= 8)
        def _():
            lax.fori_loop(0, HEADS, sums, 0)

        @pl.when(e == 13)
        def _():
            for which in range(2):
                @pl.when(2 * (z % 4) + which != z)
                def _():
                    rows = evict_rows(which, y)
                    copy(rows, rows, ezs.at[0], ezr.at[which], across).wait_recv()

            @pl.when(jnp.logical_or(z == 0, z == NZ - 1))
            def _():
                evict_own().wait()

            for which in range(2):
                for i in (1, 3, 2):
                    evict_y(which, i).start()

        return carry

    lax.fori_loop(1, 19, tick, 0)

    for h in range(HEADS):
        cols = head_cols(h)
        for side, inner in ((0, z > 0), (1, z < NZ - 1)):
            @pl.when(inner)
            def _():
                zl_copy(z, h, side, across).wait_recv()
                zo_copy(z, h, side, across).wait_recv()

        first, second, own = zl_recv[0, z, h], zl_recv[1, z, h], zl_own[z, h]
        whole = lse2(first, second, own)
        mixed = (
            zo_recv[0, z, cols, :].astype(F32) * jnp.exp2(first - whole)[0:1]
            + zo_recv[1, z, cols, :].astype(F32) * jnp.exp2(second - whole)[0:1]
            + zo_own[z, cols, :] * jnp.exp2(own - whole)[0:1]
        )
        comb[:, h * HD : (h + 1) * HD] = mixed.T[:ROWS].astype(BF)

    def return2(dev):
        return copy(comb.at[theirs, :], ret.at[zh], cs, cr, dev)

    return2(across).start()
    ret[zh] = comb[mine, :]
    part = ret.at[1 - zh]
    copy(part, part, cs, cr, across).wait_recv()
    dense[0, 0] = ret[0].astype(F32)
    dense[1, 0] = ret[1].astype(F32)

    def return1(other):
        return copy(
            packb.at[other, pl.ds(0, BACK1), :], recv2.at[xc], ds.at[other], dr.at[xc],
            beside(other),
        )

    def return1_wait(other):
        part = recv2.at[other]
        copy(part, part, ds.at[other], dr.at[other], beside(other)).wait_recv()

    for i in range(1, NXC):
        step1((xc + i) % NXC).wait_send()
    for d in range(NXC):
        for half in range(2):
            for h in range(HEADS):
                row = (half * HEADS + h) * TOK
                pack32[d, row : row + TOK, :] = dense[
                    half, 0, d * TOK : (d + 1) * TOK, h * HD : (h + 1) * HD
                ]
        packb[d, 0:BACK1, :] = pack32[d, 0:BACK1, :].astype(BF)
    for i in range(1, NXC):
        return1((xc + i) % NXC).start()
    recv2[xc] = packb[xc, 0:BACK1, :]
    for i in range(1, NXC):
        return1_wait((xc + i) % NXC)
    for s in range(NXC):
        pack32[s, 0:BACK1, :] = recv2[s].astype(F32)
        for half in range(2):
            for h in range(HEADS):
                row = (half * HEADS + h) * TOK
                col = ((half * NXC + s) * HEADS + h) * HD
                out_ref[:, col : col + HD] = pack32[s, row : row + TOK, :]

    for which in range(2):
        for i in (1, 3, 2):
            evict_y_wait(which, i)
    return2(across).wait_send()
    step2(0, 1).wait_send()
    step2(1, 2).wait_send()
    for i in range(1, NXC):
        return1((xc + i) % NXC).wait_send()
    for i in (1, 2, 3):
        a_copy(i).wait_send()
        for which in range(2):
            evict_y(which, i).wait_send()
        for h in range(HEADS):
            k_copy(h, i).wait_send()
            v_copy(h, i).wait_send()
    for half in range(2):
        @pl.when(z // 2 + 4 * half != z)
        def _():
            evict_z(half).wait_send()

    def drain(block, carry):
        for h in range(HEADS):
            @pl.when(jnp.logical_and(block <= z, z < NZ - 1))
            def _():
                z_copy(block, h, 0).wait_send()

            @pl.when(jnp.logical_and(block >= z, z > 0))
            def _():
                z_copy(block, h, 1).wait_send()

            @pl.when(block != z)
            def _():
                zl_copy(block, h, 0, across).wait_send()
                zo_copy(block, h, 0, across).wait_send()

        return carry

    lax.fori_loop(0, NZ, drain, 0)


def attention(x, window, owner, oldest, slopes):
    dma = pltpu.SemaphoreType.DMA
    vm = pltpu.VMEM
    in_vmem = pl.BlockSpec(memory_space=pltpu.VMEM)
    in_smem = pl.BlockSpec(memory_space=pltpu.SMEM)
    return pl.pallas_call(
        kernel,
        out_shape=(
            jax.ShapeDtypeStruct((TOK, 2 * NXC * SHARE), F32),
            jax.ShapeDtypeStruct((2, CACHE, SHARE), BF),
        ),
        in_specs=[in_vmem, in_vmem, in_smem, in_smem, in_smem],
        out_specs=(in_vmem, pl.BlockSpec(memory_space=pl.ANY)),
        scratch_shapes=[
            vm((NXC, OUT1, HD), F32),
            vm((NXC, OUT1, HD), BF),
            vm((NXC, OUT1, HD), BF),
            vm((2, 3, HALF, SHARE), F32),
            vm((3, ROWS, SHARE), BF),
            vm((NZ, ROWS, SHARE), BF),
            vm((NY, HEADS, CACHE, HD), BF),
            vm((NY, HEADS, SUMS, CACHE), BF),
            vm((NY, 2, ROWS, SHARE), BF),
            vm((HEADS, SUMS, PACK), BF),
            vm((SUMS, PACK), F32),
            vm((NZ, SHARE, HD), F32),
            vm((2, NZ, SHARE, HD), BF),
            vm((NZ, SHARE, HD), BF),
            vm((NZ, HEADS, 8, HD), F32),
            vm((2, NZ, HEADS, 8, HD), F32),
            vm((NZ, HEADS, 8, HD), F32),
            vm((ROWS, SHARE), BF),
            vm((3, HALF, SHARE), BF),
            vm((2, HALF, SHARE), BF),
            vm((NXC, BACK1, HD), BF),
            dma((NXC,)), dma((NXC,)),
            dma((3,)), dma((3,)),
            dma((2, NZ, HEADS)), dma((NZ, HEADS)),
            dma((NY, HEADS)), dma((NY, HEADS)), dma((NY, HEADS)), dma((NY, HEADS)),
            dma((NY,)), dma((NY,)),
            dma((NZ, HEADS)), dma((2, NZ, HEADS)), dma((NZ, HEADS)), dma((2, NZ, HEADS)),
            dma((2,)), dma((2,)), dma((2, NY)), dma((2, NY)),
            dma(()), dma(()), dma((NXC,)), dma((NXC,)), dma(()),
        ],
        compiler_params=pltpu.CompilerParams(
            collective_id=0, has_side_effects=True, vmem_limit_bytes=48 * 1024 * 1024
        ),
        cost_estimate=pl.CostEstimate(
            flops=4 * 3072 * 864 * SHARE, bytes_accessed=4 * 2**20, transcendentals=3072 * 864 * 3
        ),
    )(x, window, owner, oldest, slopes)


def body(active_qkv, window_kv, slot_owner, oldest_slot, timestep, time_slopes, gate_table):
    combined, moved = attention(active_qkv, window_kv, slot_owner, oldest_slot, time_slopes)
    my_slot = lax.dynamic_slice_in_dim(slot_owner, lax.axis_index("grp"), 1, 0)[0]
    new_window = jnp.where(my_slot == oldest_slot[0], moved, window_kv)
    gate = lax.dynamic_slice_in_dim(gate_table, timestep[0], 1, 0)
    return ((gate * combined).astype(BF), new_window)


def solution(mesh):
    in_specs = (P(None, ("grp", "sp"), None), P(None, "grp", "sp"), P(), P(), P(), P(), P())
    out_specs = (P(("grp", "sp"), None), P(None, "grp", "sp"))
    return jax.shard_map(body, mesh=mesh, in_specs=in_specs, out_specs=out_specs, check_vma=False)
```

time: 663 us -> 133 us (0.20)
  the two profiles are of different devices: /device:TPU:6 before, /device:TPU:1 now
where the time goes in v2:
time: 133 us
  Pallas kernels  124 us (93%)
  local copies, waits for them, and re-layouts  4.82 us (4%)
  between operations  2.73 us (2%)
  other arithmetic  1.85 us (1%)
    pallas_call x1, Pallas kernels, attention(): pl.pallas_call(kernel, out_shape=(jax.ShapeDtypeStruct((TOK, 2 * NXC * SH...  124 us
    unnamed x10, local copies, waits for them, and re-layouts  3.55 us

profile of v2, /device:TPU:1, one launch (start us, length us, event | category | flops | bytes accessed | tf_op | source)
XLA Modules:
  0.0 133.2 jit_solution(17580381146224038838)
XLA Ops:
  0.6 0.0 copy-start
  2.1 1.2 dynamic_slice.7
  3.9 0.0 copy-done
  4.0 0.0 copy-start.1
  4.0 1.3 copy-done.1
  5.3 0.0 copy-start.2
  5.3 1.0 copy-done.2
  6.2 0.0 copy-start.3
  6.2 0.7 copy-done.3
  6.9 0.0 copy-start.4
  6.9 0.7 copy-done.4
  7.5 123.8 %shard_map.86 = (f32[6,6144]{1,0:T(8,128)S(1)}, bf16[2,768,384]{2,1,0:T(8,128)(2,1)S(1)}) custom-call(bf16[3,6,6144]{2,1,0:T(8,128)(2,1)S(1)} %copy-done.2, bf16[2,768,384]{2,1,0:T(8,128)(2,1)S(1)} %copy-done.1, s32[32]{0:T(128)S(1)} %copy-done.3, s32[1]{0:T(128)S(6)} %copy.9.oldest_ref, f32[48]{0:T(128)S(1)} %copy-done.4), custom_call_target="tpu_custom_call" | custom-call | flops 4076863488 | bytes 4194304 | tf_op jit(solution)/shard_map/pallas_call | solution.py:523
  131.3 0.7 multiply_convert_fusion
  132.0 1.2 broadcast_select_fusion
  (1 shorter events, 0.0 us)
Async XLA Ops:
  0.6 3.3 %copy-start = (f32[50,6144]{1,0:T(8,128)S(1)}, f32[50,6144]{1,0:T(8,128)}, u32[]{:S(2)}) copy-start(f32[50,6144]{1,0:T(8,128)} %param.13) | copy-start | bytes 3686404
  4.0 1.3 copy-start.1
  5.3 1.0 copy-start.2
  6.2 0.7 copy-start.3
  6.9 0.7 copy-start.4

commit v3 on v2

v3 whole, which is shorter than its diff:
```python
import functools
import math

import jax
import jax.numpy as jnp
from jax import lax
from jax.experimental import pallas as pl
from jax.experimental.pallas import tpu as pltpu
from jax.sharding import PartitionSpec as P

HD = 128
WIN = 8
HEADS = 3
SHARE = HEADS * HD
TOK = 6
ROWS = 96
HALF = 48
CACHE = 768
NZ = 8
NY = 4
NXC = 8
PACK = 4 * ROWS
OUT1 = 112
BACK1 = 48
SUMS = HD + 16
LOG2E = math.log2(math.e)
COEF = LOG2E / math.sqrt(HD)
NONE = -1e30
MESH = pl.DeviceIdType.MESH
BF = jnp.bfloat16
F32 = jnp.float32
NT = (((1,), (1,)), ((), ()))


def lse2(*parts):
    top = functools.reduce(jnp.maximum, parts)
    return top + jnp.log2(sum(jnp.exp2(p - top) for p in parts))


def kernel(
    x_hbm, win_ref, owner_hbm, oldest_hbm, slope_hbm, out_ref, moved_ref, flag_ref,
    x_ref, vbuf, owner_ref, oldest_ref, slope_ref, in_sem,
    pack32, packb, recv1, dense, local, qbuf, kbuf, vt, akv, vta, acc_ref, top_ref,
    so, sl, qo, ql, mo, ml, fo, fl, back, recv2,
    s1s, s1r, s2s, s2r, zsend, zrecv, ks, kr, vs, vr, k2s, k2r, v2s, v2r, acs, acr, a2s, a2r,
    qos, qor, qls, qlr, fos, for_, fls, flr, ezs, ezr, eys, eyr, e2s, e2r, ds, dr, cp_sem,
):
    me = lax.axis_index("grp")
    sp = lax.axis_index("sp")
    z = me // NY
    y = me % NY
    zh = sp // NXC
    xc = sp % NXC
    quad = z // 4
    seat = z % 4

    def at(zz, yy):
        return {"grp": zz * NY + yy, "sp": sp}

    def beside(other):
        return {"grp": me, "sp": zh * NXC + other}

    across = {"grp": me, "sp": (1 - zh) * NXC + xc}
    over = (z + 4) % NZ
    across_over = {"grp": over * NY + y, "sp": (1 - zh) * NXC + xc}

    def copy(src, dst, send, recv, dev):
        return pltpu.make_async_remote_copy(
            src_ref=src, dst_ref=dst, send_sem=send, recv_sem=recv,
            device_id=dev, device_id_type=MESH,
        )

    def head_cols(h):
        return pl.ds(pl.multiple_of(h * HD, HD), HD)

    loads = [
        pltpu.make_async_copy(src, dst, in_sem.at[i])
        for i, (src, dst) in enumerate(
            [
                (x_hbm, x_ref), (win_ref.at[1], vbuf), (owner_hbm, owner_ref),
                (oldest_hbm, oldest_ref), (slope_hbm, slope_ref),
            ]
            + [(win_ref.at[0, :, h * HD : (h + 1) * HD], kbuf.at[y, h]) for h in range(HEADS)]
        )
    ]
    for load in loads:
        load.start()

    barrier = pltpu.get_barrier_semaphore()
    peers = [at((z + i) % NZ, y) for i in range(1, NZ)]
    peers += [at(z, (y + i) % NY) for i in range(1, NY)]
    peers += [beside((xc + i) % NXC) for i in range(1, NXC)]
    peers += [across, across_over]
    for peer in peers:
        pl.semaphore_signal(barrier, inc=1, device_id=peer, device_id_type=MESH)
    pl.semaphore_wait(barrier, len(peers))

    def k_copy(h, i):
        return copy(
            win_ref.at[0, :, h * HD : (h + 1) * HD], kbuf.at[y, h], ks.at[i, h], kr.at[i, h],
            at(z, (y + i) % NY),
        )

    def v_copy(h, i):
        return copy(
            vt.at[y, h, pl.ds(0, HD), :], vt.at[y, h, pl.ds(0, HD), :], vs.at[i, h], vr.at[i, h],
            at(z, (y + i) % NY),
        )

    def kv_wait(h, i):
        src = (y + NY - i) % NY
        copy(kbuf.at[src, h], kbuf.at[src, h], ks.at[i, h], kr.at[i, h], at(z, src)).wait_recv()
        rows = vt.at[src, h, pl.ds(0, HD), :]
        copy(rows, rows, vs.at[i, h], vr.at[i, h], at(z, src)).wait_recv()

    def halves(src, h, part):
        rows = pl.ds(part * PACK, PACK)
        return kbuf.at[src, h, rows, :], vt.at[src, h, pl.ds(0, HD), rows]

    def relay_copies(src, h, part):
        dev = at(z, (y + 1 + 2 * part) % NY)
        keys, values = halves(src, h, part)
        return (
            copy(keys, keys, k2s.at[part, h], k2r.at[part, h], dev),
            copy(values, values, v2s.at[part, h], v2r.at[part, h], dev),
        )

    def relay(h):
        for part, i in ((0, 1), (1, 3)):
            kv_wait(h, i)
            for each in relay_copies((y + NY - i) % NY, h, part):
                each.start()

    def relay_wait(h, part):
        for each in relay_copies((y + 2) % NY, h, part):
            each.wait_recv()

    for i in (1, 3):
        k_copy(0, i).start()

    def step1(other):
        return copy(packb.at[other], recv1.at[xc], s1s.at[other], s1r.at[xc], beside(other))

    def step1_wait(other):
        copy(recv1.at[other], recv1.at[other], s1s.at[other], s1r.at[other], beside(other)).wait_recv()

    def piece(half, t, h):
        return half * 54 + (t * HEADS + h) * TOK

    loads[0].wait()
    for d in range(NXC):
        for half in range(2):
            for t in range(3):
                for h in range(HEADS):
                    col = ((half * NXC + d) * HEADS + h) * HD
                    row = piece(half, t, h)
                    pack32[d, row : row + TOK, :] = x_ref[t, :, col : col + HD].astype(F32)
        packb[d] = pack32[d].astype(BF)
    for i in range(1, NXC):
        step1((xc + i) % NXC).start()
    recv1[xc] = packb[xc]

    loads[1].wait()
    for h in range(HEADS):
        vt[y, h, 0:HD, :] = vbuf[:, h * HD : (h + 1) * HD].astype(F32).T.astype(BF)
        if h < 2:
            for i in (1, 3):
                v_copy(h, i).start()
        if h == 0:
            for i in (1, 3):
                k_copy(1, i).start()
        for src in range(NY):
            vt[src, h, HD:SUMS, :] = jnp.ones((SUMS - HD, CACHE), BF)
        vta[h, HD:SUMS, :] = jnp.ones((SUMS - HD, PACK), BF)
    for load in loads[2:]:
        load.wait()
    flag_ref[...] = jnp.full((8, HD), (owner_ref[me] == oldest_ref[0]).astype(F32))

    theirs = pl.ds(pl.multiple_of((1 - zh) * HALF, HALF), HALF)
    for h in range(HEADS):
        for i in range(4):
            qo[h, i, :, ROWS:HD, :] = jnp.zeros((2, HD - ROWS, HD), BF)
        for half in range(2):
            fo[half, h, :, ROWS:HD, :] = jnp.zeros((2, HD - ROWS, HD), BF)
            fo[half, h, :, theirs, :] = jnp.zeros((2, HALF, HD), BF)

    for i in range(1, NXC):
        step1_wait((xc + i) % NXC)
    for s in range(NXC):
        pack32[s] = recv1[s].astype(F32)
    for t in range(3):
        for s in range(NXC):
            for half in range(2):
                for h in range(HEADS):
                    row = piece(half, t, h)
                    dense[half, t, s * TOK : (s + 1) * TOK, h * HD : (h + 1) * HD] = pack32[
                        s, row : row + TOK, :
                    ]

    mine = pl.ds(pl.multiple_of(zh * HALF, HALF), HALF)

    def step2(t, n):
        part = back.at[pl.ds(t, n)]
        return copy(part, local.at[pl.ds(t, n), mine, :], s2s.at[t], s2r.at[t], across)

    def step2_wait(t, n):
        part = local.at[pl.ds(t, n), theirs, :]
        copy(part, part, s2s.at[t], s2r.at[t], across).wait_recv()

    back[0] = dense[1 - zh, 0].astype(BF)
    step2(0, 1).start()
    for t in (1, 2):
        back[t] = dense[1 - zh, t].astype(BF)
    step2(1, 2).start()
    for t in range(3):
        local[t, mine, :] = dense[zh, t].astype(BF)

    def z_copy(block, h, side):
        part = qbuf.at[block, :, head_cols(h)]
        return copy(
            part, part, zsend.at[side, block, h], zrecv.at[block, h], at(z + 1 - 2 * side, y)
        )

    def z_wait(block, h):
        part = qbuf.at[block, :, head_cols(h)]
        copy(part, part, zsend.at[0, block, h], zrecv.at[block, h], across).wait_recv()

    step2_wait(0, 1)
    qbuf[z] = local[0]
    for h in range(HEADS):
        @pl.when(z < NZ - 1)
        def _():
            z_copy(z, h, 0).start()

        @pl.when(z > 0)
        def _():
            z_copy(z, h, 1).start()

    def gather_step(t):
        for h in range(HEADS):
            @pl.when(z - t >= 0)
            def _():
                z_wait(z - t, h)

                @pl.when(z < NZ - 1)
                def _():
                    z_copy(z - t, h, 0).start()

            @pl.when(z + t < NZ)
            def _():
                z_wait(z + t, h)

                @pl.when(z > 0)
                def _():
                    z_copy(z + t, h, 1).start()

    def a_copy(i):
        return copy(akv.at[y], akv.at[y], acs.at[i], acr.at[i], at(z, (y + i) % NY))

    def a_wait(i):
        src = (y + NY - i) % NY
        copy(akv.at[src], akv.at[src], acs.at[i], acr.at[i], at(z, src)).wait_recv()

    def a_relay(src, part):
        rows = akv.at[src, part]
        return copy(rows, rows, a2s.at[part], a2r.at[part], at(z, (y + 1 + 2 * part) % NY))

    def evict_rows(which, column):
        return moved_ref.at[:, pl.ds((which * NY + column) * ROWS, ROWS), :]

    def evict_z(half):
        return copy(
            akv.at[y], evict_rows(z % 2, y), ezs.at[half], ezr.at[z % 2], at(z // 2 + 4 * half, y)
        )

    def evict_own():
        return pltpu.make_async_copy(akv.at[y], evict_rows(z % 2, y), cp_sem)

    def evict_y(which, i):
        rows = evict_rows(which, y)
        return copy(rows, rows, eys.at[which, i], eyr.at[which, i], at(z, (y + i) % NY))

    def evict_relay(which, src):
        rows = evict_rows(which, src)
        return copy(rows, rows, e2s.at[which], e2r.at[which], at(z, (y + 1 + 2 * which) % NY))

    def evict_y_wait(which, i):
        src = (y + NY - i) % NY
        rows = evict_rows(which, src)
        copy(rows, rows, eys.at[which, i], eyr.at[which, i], at(z, src)).wait_recv()

    def attend(h, sources, start, stop):
        cols = head_cols(h)
        q = qbuf[:, :, cols].reshape(NZ * ROWS, HD)
        slope = slope_ref[sp * HEADS + h] * LOG2E

        def window(i, part):
            src = (y + NY - i) % NY
            rows = slice(part * PACK, (part + 1) * PACK)
            slot = owner_ref[z * NY + src] - oldest_ref[0]
            age = WIN - (slot + WIN) % WIN
            return kbuf[src, h, rows, :], vt.at[src, h, :, rows], slope * age.astype(F32)

        chunks = [(akv[:, 0, :, cols].reshape(PACK, HD), vta.at[h], None)] if start else []
        chunks += [window(i, part) for i in sources for part in range(2)]
        top, acc = (None, None) if start else (top_ref[0:1, :], acc_ref[...])
        ahead = lax.dot_general(chunks[0][0], q, NT, preferred_element_type=F32)
        for n, (_, values, bias) in enumerate(chunks):
            score = ahead
            if n + 1 < len(chunks):
                ahead = lax.dot_general(chunks[n + 1][0], q, NT, preferred_element_type=F32)
            new = jnp.max(score, axis=0, keepdims=True) * COEF
            if bias is not None:
                new = new - bias
            if top is not None:
                new = jnp.maximum(top, new)
            weight = jnp.exp2(score * COEF - (new if bias is None else new + bias))
            part = jnp.dot(values[...], weight.astype(BF), preferred_element_type=F32)
            acc = part if top is None else acc * jnp.exp2(top - new) + part
            top = new
        if not stop:
            top_ref[...] = jnp.broadcast_to(top, (8, NZ * ROWS))
            acc_ref[...] = acc
            return
        total = acc[HD : HD + 1]
        mixed = acc[:HD] * (1.0 / total)
        lse = jnp.broadcast_to(top + jnp.log2(total), (8, NZ * ROWS))
        for j in range(NZ):
            pack = slice(j // 4 * PACK, (j // 4 + 1) * PACK)
            tokens, sums = mixed[:, pack], lse[:, pack]
            if j % 4:
                tokens = pltpu.roll(tokens, PACK - ROWS * (j % 4), 1)
                sums = pltpu.roll(sums, PACK - ROWS * (j % 4), 1)
            so[h, j % 4, j // 4] = tokens[:, :HD].T[:ROWS].astype(BF)
            sl[h, j % 4, 4 * (j // 4) : 4 * (j // 4) + 4, :] = sums[:4, :HD]

    def quad_copies(h, other):
        dev = at(quad * 4 + other, y)
        return (
            copy(sl.at[h, other], ql.at[h, seat], qls.at[h, other], qlr.at[h, seat], dev),
            copy(
                so.at[h, other], qo.at[h, seat, :, pl.ds(0, ROWS), :], qos.at[h, other],
                qor.at[h, seat], dev,
            ),
        )

    def quad_wait(h, other):
        part = ql.at[h, other]
        copy(part, part, qls.at[h, other], qlr.at[h, other], across).wait_recv()
        part = qo.at[h, other, :, pl.ds(0, ROWS), :]
        copy(part, part, qos.at[h, other], qor.at[h, other], across).wait_recv()

    def to_quad(h):
        for i in (3, 2, 1):
            for each in quad_copies(h, (seat + i) % 4):
                each.start()
        ql[h, seat] = sl[h, seat]
        qo[h, seat, :, 0:ROWS, :] = so[h, seat]

    def spread(weight, first_row, rows):
        at_row = lax.broadcasted_iota(jnp.int32, (rows, HD), 0) + first_row
        at_col = lax.broadcasted_iota(jnp.int32, (rows, HD), 1)
        return jnp.where(at_row == at_col, weight, 0.0).astype(BF)

    def final_copies(h, k, there):
        dev = (at(over, y), across, across_over)[there]
        rows = theirs if there else mine
        return (
            copy(ml.at[h, k], fl.at[zh, h, quad], fls.at[h, there], flr.at[zh, h, quad], dev),
            copy(
                mo.at[h, k, rows, :], fo.at[zh, h, quad, rows, :], fos.at[h, there],
                for_.at[zh, h, quad], dev,
            ),
        )

    ways = ((2, 1), (1, 0), (0, 1))

    def reduce(h):
        for i in (1, 2, 3):
            quad_wait(h, (seat + i) % 4)
        for k in (1, 0):
            slot = (quad + k) % 2
            row = pl.ds(slot * 4, 1)
            parts = [ql[h, i, row, :] for i in range(4)]
            whole = lse2(*parts)
            weights = jnp.concatenate(
                [spread(jnp.exp2(p - whole), 0, ROWS) for p in parts], axis=1
            )
            mo[h, k] = jnp.dot(
                weights, qo[h, :, slot].reshape(4 * HD, HD), preferred_element_type=F32
            ).astype(BF)
            ml[h, k] = jnp.broadcast_to(whole, (8, HD))
            for there, which in ways:
                if which == k:
                    for each in final_copies(h, k, there):
                        each.start()
        fl[zh, h, quad] = ml[h, 0]
        fo[zh, h, quad, mine, :] = mo[h, 0, mine, :]

    def final_wait(half, h, which):
        part = fl.at[half, h, which]
        copy(part, part, fls.at[h, 0], flr.at[half, h, which], across).wait_recv()
        part = fo.at[half, h, which, mine, :]
        copy(part, part, fos.at[h, 0], for_.at[half, h, which], across).wait_recv()

    def finish(h):
        final_wait(zh, h, 1 - quad)
        final_wait(1 - zh, h, 0)
        final_wait(1 - zh, h, 1)
        for half in range(2):
            parts = [fl[half, h, i, 0:1, :] for i in range(2)]
            whole = lse2(*parts)
            weights = jnp.concatenate(
                [spread(jnp.exp2(p - whole), zh * HALF, HALF) for p in parts], axis=1
            )
            dense[half, 0, :, h * HD : (h + 1) * HD] = jnp.dot(
                weights, fo[half, h].reshape(2 * HD, HD), preferred_element_type=F32
            )

    def gather_tick(e, carry):
        gather_step(e)

        @pl.when(e == 1)
        def _():
            relay(0)

        @pl.when(e == 2)
        def _():
            step2_wait(1, 2)
            akv[y] = local[1:3]
            for i in (1, 3):
                a_copy(i).start()

        @pl.when(e == 3)
        def _():
            for part, i in ((0, 1), (1, 3)):
                a_wait(i)
                a_relay((y + NY - i) % NY, part).start()

        @pl.when(e == 4)
        def _():
            relay(1)

        @pl.when(e == 5)
        def _():
            for i in (1, 3):
                k_copy(2, i).start()
                v_copy(2, i).start()

        return carry

    lax.fori_loop(1, NZ, gather_tick, 0)

    for half in range(2):
        @pl.when(z // 2 + 4 * half != z)
        def _():
            evict_z(half).start()

    @pl.when(jnp.logical_or(z == 0, z == NZ - 1))
    def _():
        evict_own().start()

    for part in range(2):
        a_relay((y + 2) % NY, part).wait_recv()
    for h in range(HEADS):
        values = akv[:, 1, :, h * HD : (h + 1) * HD].reshape(PACK, HD)
        vta[h, 0:HD, :] = values.astype(F32).T.astype(BF)

    def whole_head(h, carry):
        for part in range(2):
            relay_wait(h, part)
        attend(h, (0, 1, 3, 2), True, True)
        to_quad(h)
        return carry

    lax.fori_loop(0, 2, whole_head, 0)
    relay(2)
    attend(2, (0, 1, 3), True, False)
    reduce(0)
    reduce(1)
    for part in range(2):
        relay_wait(2, part)
    attend(2, (2,), False, True)
    to_quad(2)

    for which in range(2):
        @pl.when(2 * (z % 4) + which != z)
        def _():
            rows = evict_rows(which, y)
            copy(rows, rows, ezs.at[0], ezr.at[which], across).wait_recv()

    @pl.when(jnp.logical_or(z == 0, z == NZ - 1))
    def _():
        evict_own().wait()

    for which in range(2):
        for i in (1, 3):
            evict_y(which, i).start()

    finish(0)
    finish(1)
    reduce(2)
    for which, i in ((0, 1), (1, 3)):
        evict_y_wait(which, i)
        evict_relay(which, (y + NY - i) % NY).start()
    finish(2)

    def return1(other):
        return copy(
            packb.at[other, pl.ds(0, BACK1), :], recv2.at[xc], ds.at[other], dr.at[xc],
            beside(other),
        )

    def return1_wait(other):
        part = recv2.at[other]
        copy(part, part, ds.at[other], dr.at[other], beside(other)).wait_recv()

    for i in range(1, NXC):
        step1((xc + i) % NXC).wait_send()
    for d in range(NXC):
        for half in range(2):
            for h in range(HEADS):
                row = (half * HEADS + h) * TOK
                pack32[d, row : row + TOK, :] = dense[
                    half, 0, d * TOK : (d + 1) * TOK, h * HD : (h + 1) * HD
                ]
        packb[d, 0:BACK1, :] = pack32[d, 0:BACK1, :].astype(BF)
    for i in range(1, NXC):
        return1((xc + i) % NXC).start()
    recv2[xc] = packb[xc, 0:BACK1, :]
    for i in range(1, NXC):
        return1_wait((xc + i) % NXC)
    for s in range(NXC):
        pack32[s, 0:BACK1, :] = recv2[s].astype(F32)
        for half in range(2):
            for h in range(HEADS):
                row = (half * HEADS + h) * TOK
                col = ((half * NXC + s) * HEADS + h) * HD
                out_ref[:, col : col + HD] = pack32[s, row : row + TOK, :]

    evict_y_wait(1, 1)
    evict_y_wait(0, 3)
    for which in range(2):
        evict_relay(which, (y + 2) % NY).wait_recv()
    for h in range(HEADS):
        for i in (1, 2, 3):
            for each in quad_copies(h, (seat + i) % 4):
                each.wait_send()
        for there, k in ways:
            for each in final_copies(h, k, there):
                each.wait_send()
    step2(0, 1).wait_send()
    step2(1, 2).wait_send()
    for i in range(1, NXC):
        return1((xc + i) % NXC).wait_send()
    for i in (1, 3):
        a_copy(i).wait_send()
        for which in range(2):
            evict_y(which, i).wait_send()
        for h in range(HEADS):
            k_copy(h, i).wait_send()
            v_copy(h, i).wait_send()
    for part, i in ((0, 1), (1, 3)):
        src = (y + NY - i) % NY
        a_relay(src, part).wait_send()
        evict_relay(part, src).wait_send()
        for h in range(HEADS):
            for each in relay_copies(src, h, part):
                each.wait_send()
    for half in range(2):
        @pl.when(z // 2 + 4 * half != z)
        def _():
            evict_z(half).wait_send()

    def drain(block, carry):
        for h in range(HEADS):
            @pl.when(jnp.logical_and(block <= z, z < NZ - 1))
            def _():
                z_copy(block, h, 0).wait_send()

            @pl.when(jnp.logical_and(block >= z, z > 0))
            def _():
                z_copy(block, h, 1).wait_send()

        return carry

    lax.fori_loop(0, NZ, drain, 0)


def attention(x, window, owner, oldest, slopes):
    dma = pltpu.SemaphoreType.DMA
    vm = pltpu.VMEM
    in_vmem = pl.BlockSpec(memory_space=pltpu.VMEM)
    in_any = pl.BlockSpec(memory_space=pl.ANY)
    return pl.pallas_call(
        kernel,
        out_shape=(
            jax.ShapeDtypeStruct((TOK, 2 * NXC * SHARE), F32),
            jax.ShapeDtypeStruct((2, CACHE, SHARE), BF),
            jax.ShapeDtypeStruct((8, HD), F32),
        ),
        in_specs=[in_any] * 5,
        out_specs=(in_vmem, in_any, in_vmem),
        scratch_shapes=[
            vm((3, TOK, 2 * NXC * SHARE), BF),
            vm((CACHE, SHARE), BF),
            pltpu.SMEM((NZ * NY,), jnp.int32),
            pltpu.SMEM((1,), jnp.int32),
            pltpu.SMEM((2 * NXC * HEADS,), F32),
            dma((8,)),
            vm((NXC, OUT1, HD), F32),
            vm((NXC, OUT1, HD), BF),
            vm((NXC, OUT1, HD), BF),
            vm((2, 3, HALF, SHARE), F32),
            vm((3, ROWS, SHARE), BF),
            vm((NZ, ROWS, SHARE), BF),
            vm((NY, HEADS, CACHE, HD), BF),
            vm((NY, HEADS, SUMS, CACHE), BF),
            vm((NY, 2, ROWS, SHARE), BF),
            vm((HEADS, SUMS, PACK), BF),
            vm((SUMS, NZ * ROWS), F32),
            vm((8, NZ * ROWS), F32),
            vm((HEADS, 4, 2, ROWS, HD), BF),
            vm((HEADS, 4, 8, HD), F32),
            vm((HEADS, 4, 2, HD, HD), BF),
            vm((HEADS, 4, 8, HD), F32),
            vm((HEADS, 2, ROWS, HD), BF),
            vm((HEADS, 2, 8, HD), F32),
            vm((2, HEADS, 2, HD, HD), BF),
            vm((2, HEADS, 2, 8, HD), F32),
            vm((3, HALF, SHARE), BF),
            vm((NXC, BACK1, HD), BF),
            dma((NXC,)), dma((NXC,)),
            dma((3,)), dma((3,)),
            dma((2, NZ, HEADS)), dma((NZ, HEADS)),
            dma((NY, HEADS)), dma((NY, HEADS)), dma((NY, HEADS)), dma((NY, HEADS)),
            dma((2, HEADS)), dma((2, HEADS)), dma((2, HEADS)), dma((2, HEADS)),
            dma((NY,)), dma((NY,)), dma((2,)), dma((2,)),
            dma((HEADS, 4)), dma((HEADS, 4)), dma((HEADS, 4)), dma((HEADS, 4)),
            dma((HEADS, 3)), dma((2, HEADS, 2)), dma((HEADS, 3)), dma((2, HEADS, 2)),
            dma((2,)), dma((2,)), dma((2, NY)), dma((2, NY)),
            dma((2,)), dma((2,)),
            dma((NXC,)), dma((NXC,)), dma(()),
        ],
        compiler_params=pltpu.CompilerParams(
            collective_id=0, has_side_effects=True, vmem_limit_bytes=60 * 1024 * 1024
        ),
        cost_estimate=pl.CostEstimate(
            flops=4 * 3072 * 864 * SHARE, bytes_accessed=4 * 2**20, transcendentals=3072 * 864 * 3
        ),
    )(x, window, owner, oldest, slopes)


def body(active_qkv, window_kv, slot_owner, oldest_slot, timestep, time_slopes, gate_table):
    combined, moved, flag = attention(active_qkv, window_kv, slot_owner, oldest_slot, time_slopes)
    new_window = jnp.where(flag[0, 0] > 0, moved, window_kv)
    gate = lax.dynamic_slice_in_dim(gate_table, timestep[0], 1, 0)
    return ((gate * combined).astype(BF), new_window)


def solution(mesh):
    in_specs = (P(None, ("grp", "sp"), None), P(None, "grp", "sp"), P(), P(), P(), P(), P())
    out_specs = (P(("grp", "sp"), None), P(None, "grp", "sp"))
    return jax.shard_map(body, mesh=mesh, in_specs=in_specs, out_specs=out_specs, check_vma=False)
```

time: 133 us -> 108 us (0.81)
  Pallas kernels: 124 us -> 101 us
  local copies, waits for them, and re-layouts: 4.82 us -> 1.23 us
    pallas_call x1, Pallas kernels: 124 us -> 101 us  [attention(): pl.pallas_call(kernel, out_shape=(jax.ShapeDtypeStruct((TOK, 2 * NXC * SH...]
    unnamed x10 -> x4, local copies, waits for them, and re-layouts: 3.55 us -> 0.02 us
where the time goes in v3:
time: 108 us
  Pallas kernels  101 us (94%)
  other arithmetic  2.75 us (3%)
  between operations  2.73 us (3%)
  local copies, waits for them, and re-layouts  1.23 us (1%)
    pallas_call x1, Pallas kernels, attention(): pl.pallas_call(kernel, out_shape=(jax.ShapeDtypeStruct((TOK, 2 * NXC * SH...  101 us

profile of v3, /device:TPU:1, one launch (start us, length us, event | category | flops | bytes accessed | tf_op | source)
XLA Modules:
  0.0 107.8 jit_solution(8612103930721534417)
XLA Ops:
  0.6 0.0 copy-start
  2.0 0.0 copy-done
  2.1 0.0 copy-start.1
  2.1 101.1 %shard_map.86 = (f32[6,6144]{1,0:T(8,128)}, bf16[2,768,384]{2,1,0:T(8,128)(2,1)}, f32[8,128]{1,0:T(8,128)}) custom-call(bf16[3,6,6144]{2,1,0:T(8,128)(2,1)} %x_hbm.1, bf16[2,768,384]{2,1,0:T(8,128)(2,1)} %win_ref.1, s32[32]{0:T(128)} %owner_hbm.1, s32[1]{0:T(128)S(6)} %copy.9.oldest_hbm, f32[48]{0:T(128)} %slope_hbm.1), custom_call_target="tpu_custom_call" | custom-call | flops 4076863488 | bytes 4194304 | tf_op jit(solution)/shard_map/pallas_call | solution.py:595
  103.2 1.2 %slice.3 = f32[1,1]{1,0:T(1,128)} slice(f32[8,128]{1,0:T(8,128)} %get-tuple-element.6), slice={[0:1], [0:1]} | slice | bytes 8 | tf_op jit(solution)/shard_map/slice | solution.py:656
  105.1 1.6 %multiply_convert_fusion = bf16[6,6144]{1,0:T(8,128)(2,1)} fusion(f32[6,6144]{1,0:T(8,128)} %get-tuple-element.5, f32[6144]{0:T(1024)S(1)} %bitcast.6), kind=kLoop, calls=%fused_computation.1 | loop fusion | flops 73728 | bytes 245760 | tf_op jit(solution)/shard_map/convert_element_type | solution.py:658
  106.6 0.0 copy-done.1
  106.7 1.2 %broadcast_select_fusion = bf16[2,768,384]{2,1,0:T(8,128)(2,1)} fusion(bf16[2,768,384]{2,1,0:T(8,128)(2,1)} %get-tuple-element.7, bf16[2,768,384]{2,1,0:T(8,128)(2,1)S(1)} %copy-done.1, pred[]{:T(512)} %bitcast.2), kind=kLoop, calls=%fused_computation | loop fusion | flops 589824 | bytes 3538945 | tf_op jit(solution)/shard_map/jit(_where)/select_n | solution.py:656
  (1 shorter events, 0.0 us)
Async XLA Ops:
  0.6 1.4 %copy-start = (f32[50,6144]{1,0:T(8,128)S(1)}, f32[50,6144]{1,0:T(8,128)}, u32[]{:S(2)}) copy-start(f32[50,6144]{1,0:T(8,128)} %param.13) | copy-start | bytes 3686404
  2.1 104.6 %copy-start.1 = (bf16[2,768,384]{2,1,0:T(8,128)(2,1)S(1)}, bf16[2,768,384]{2,1,0:T(8,128)(2,1)}, u32[]{:S(2)}) copy-start(bf16[2,768,384]{2,1,0:T(8,128)(2,1)} %win_ref.1) | copy-start | bytes 3538948

commit v4 on v3

--- a/solution.py
+++ b/solution.py
@@ -40,9 +40,9 @@
 def kernel(
     x_hbm, win_ref, owner_hbm, oldest_hbm, slope_hbm, out_ref, moved_ref, flag_ref,
     x_ref, vbuf, owner_ref, oldest_ref, slope_ref, in_sem,
-    pack32, packb, recv1, dense, local, qbuf, kbuf, vt, akv, vta, acc_ref, top_ref,
+    pack32, packb, recv1, dense, qbuf, kbuf, vt, akv, vta, acc_ref, top_ref,
     so, sl, qo, ql, mo, ml, fo, fl, back, recv2,
-    s1s, s1r, s2s, s2r, zsend, zrecv, ks, kr, vs, vr, k2s, k2r, v2s, v2r, acs, acr, a2s, a2r,
+    s1s, s1r, s2s, s2r, sas, sar, sbs, sbr, ks, kr, vs, vr, k2s, k2r, v2s, v2r, acs, acr, a2s, a2r,
     qos, qor, qls, qlr, fos, for_, fls, flr, ezs, ezr, eys, eyr, e2s, e2r, ds, dr, cp_sem,
 ):
     me = lax.axis_index("grp")
@@ -174,7 +174,7 @@
         vta[h, HD:SUMS, :] = jnp.ones((SUMS - HD, PACK), BF)
     for load in loads[2:]:
         load.wait()
-    flag_ref[...] = jnp.full((8, HD), (owner_ref[me] == oldest_ref[0]).astype(F32))
+    flag_ref[...] = jnp.full((1, SHARE), (owner_ref[me] == oldest_ref[0]).astype(F32))
 
     theirs = pl.ds(pl.multiple_of((1 - zh) * HALF, HALF), HALF)
     for h in range(HEADS):
@@ -199,60 +199,48 @@
 
     mine = pl.ds(pl.multiple_of(zh * HALF, HALF), HALF)
 
-    def step2(t, n):
-        part = back.at[pl.ds(t, n)]
-        return copy(part, local.at[pl.ds(t, n), mine, :], s2s.at[t], s2r.at[t], across)
-
-    def step2_wait(t, n):
-        part = local.at[pl.ds(t, n), theirs, :]
-        copy(part, part, s2s.at[t], s2r.at[t], across).wait_recv()
+    def seat_copy(i):
+        src = back.at[0] if i else qbuf.at[z, mine, :]
+        dev = (at(over, y), across, across_over)[i]
+        return copy(src, qbuf.at[z, mine, :], sas.at[i], sar.at[i], dev)
+
+    def held(i):
+        return qbuf.at[
+            (over, z, over, z)[i], (mine, theirs, theirs, mine)[i], :
+        ]
+
+    def seat_wait(i):
+        copy(held(i), held(i), sas.at[i], sar.at[i], across).wait_recv()
+
+    def quad_query(i, other):
+        return copy(
+            held(i), held(i), sbs.at[i, other], sbr.at[i, seat], at(quad * 4 + other, y)
+        )
+
+    def quad_query_wait(i, other):
+        block = ((1 - quad, quad, 1 - quad, quad)[i]) * 4 + other
+        part = qbuf.at[block, (mine, theirs, theirs, mine)[i], :]
+        copy(part, part, sbs.at[i, other], sbr.at[i, other], across).wait_recv()
+
+    def pass_on(i):
+        for k in (2, 1, 3):
+            quad_query(i, (seat + k) % 4).start()
 
     back[0] = dense[1 - zh, 0].astype(BF)
-    step2(0, 1).start()
+    seat_copy(1).start()
+    seat_copy(2).start()
+    qbuf[z, mine, :] = dense[zh, 0].astype(BF)
+    seat_copy(0).start()
+    pass_on(3)
+
+    def step2():
+        return copy(back.at[pl.ds(1, 2)], akv.at[y, :, mine, :], s2s, s2r, across_over)
+
     for t in (1, 2):
         back[t] = dense[1 - zh, t].astype(BF)
-    step2(1, 2).start()
-    for t in range(3):
-        local[t, mine, :] = dense[zh, t].astype(BF)
-
-    def z_copy(block, h, side):
-        part = qbuf.at[block, :, head_cols(h)]
-        return copy(
-            part, part, zsend.at[side, block, h], zrecv.at[block, h], at(z + 1 - 2 * side, y)
-        )
-
-    def z_wait(block, h):
-        part = qbuf.at[block, :, head_cols(h)]
-        copy(part, part, zsend.at[0, block, h], zrecv.at[block, h], across).wait_recv()
-
-    step2_wait(0, 1)
-    qbuf[z] = local[0]
-    for h in range(HEADS):
-        @pl.when(z < NZ - 1)
-        def _():
-            z_copy(z, h, 0).start()
-
-        @pl.when(z > 0)
-        def _():
-            z_copy(z, h, 1).start()
-
-    def gather_step(t):
-        for h in range(HEADS):
-            @pl.when(z - t >= 0)
-            def _():
-                z_wait(z - t, h)
-
-                @pl.when(z < NZ - 1)
-                def _():
-                    z_copy(z - t, h, 0).start()
-
-            @pl.when(z + t < NZ)
-            def _():
-                z_wait(z + t, h)
-
-                @pl.when(z > 0)
-                def _():
-                    z_copy(z + t, h, 1).start()
+    step2().start()
+    for t in (1, 2):
+        akv[y, t - 1, mine, :] = dense[zh, t].astype(BF)
 
     def a_copy(i):
         return copy(akv.at[y], akv.at[y], acs.at[i], acr.at[i], at(z, (y + i) % NY))
@@ -268,13 +256,34 @@
     def evict_rows(which, column):
         return moved_ref.at[:, pl.ds((which * NY + column) * ROWS, ROWS), :]
 
-    def evict_z(half):
+    def evict_part(g):
+        base = pl.multiple_of(((z % 2) * NY + y) * ROWS, ROWS)
+        place = (zh if g == 0 else 1 - zh) * HALF
+        return (
+            akv.at[y, :, theirs if g else mine, :],
+            moved_ref.at[:, pl.ds(pl.multiple_of(base + place, HALF), HALF), :],
+        )
+
+    def evict_target(g, half):
+        return (over if g else z) // 2 + 4 * half
+
+    def evict_z(g, half):
+        src, dst = evict_part(g)
         return copy(
-            akv.at[y], evict_rows(z % 2, y), ezs.at[half], ezr.at[z % 2], at(z // 2 + 4 * half, y)
-        )
-
-    def evict_own():
-        return pltpu.make_async_copy(akv.at[y], evict_rows(z % 2, y), cp_sem)
+            src, dst, ezs.at[g, half], ezr.at[z % 2, g], at(evict_target(g, half), y)
+        )
+
+    def evict_own(g):
+        src, dst = evict_part(g)
+        return pltpu.make_async_copy(src, dst, cp_sem)
+
+    def evict_z_wait(which, g):
+        group = 2 * seat + which
+
+        @pl.when(group != (over if g else z))
+        def _():
+            part = akv.at[y, :, mine, :]
+            copy(part, part, ezs.at[0, 0], ezr.at[which, g], across).wait_recv()
 
     def evict_y(which, i):
         rows = evict_rows(which, y)
@@ -417,48 +426,37 @@
                 weights, fo[half, h].reshape(2 * HD, HD), preferred_element_type=F32
             )
 
-    def gather_tick(e, carry):
-        gather_step(e)
-
-        @pl.when(e == 1)
-        def _():
-            relay(0)
-
-        @pl.when(e == 2)
-        def _():
-            step2_wait(1, 2)
-            akv[y] = local[1:3]
-            for i in (1, 3):
-                a_copy(i).start()
-
-        @pl.when(e == 3)
-        def _():
-            for part, i in ((0, 1), (1, 3)):
-                a_wait(i)
-                a_relay((y + NY - i) % NY, part).start()
-
-        @pl.when(e == 4)
-        def _():
-            relay(1)
-
-        @pl.when(e == 5)
-        def _():
-            for i in (1, 3):
-                k_copy(2, i).start()
-                v_copy(2, i).start()
-
-        return carry
-
-    lax.fori_loop(1, NZ, gather_tick, 0)
-
-    for half in range(2):
-        @pl.when(z // 2 + 4 * half != z)
-        def _():
-            evict_z(half).start()
-
-    @pl.when(jnp.logical_or(z == 0, z == NZ - 1))
-    def _():
-        evict_own().start()
+    seat_wait(0)
+    pass_on(0)
+    seat_wait(2)
+    pass_on(2)
+    relay(0)
+    seat_wait(1)
+    pass_on(1)
+    part = akv.at[y, :, theirs, :]
+    copy(part, part, s2s, s2r, across).wait_recv()
+    for i in (1, 3):
+        a_copy(i).start()
+    for part, i in ((0, 1), (1, 3)):
+        a_wait(i)
+        a_relay((y + NY - i) % NY, part).start()
+    relay(1)
+    for i in (1, 3):
+        k_copy(2, i).start()
+        v_copy(2, i).start()
+    for i in (3, 0, 2, 1):
+        for k in (1, 2, 3):
+            quad_query_wait(i, (seat + k) % 4)
+
+    for g in range(2):
+        for half in range(2):
+            @pl.when(evict_target(g, half) != z)
+            def _():
+                evict_z(g, half).start()
+
+            @pl.when(evict_target(g, half) == z)
+            def _():
+                evict_own(g).start()
 
     for part in range(2):
         a_relay((y + 2) % NY, part).wait_recv()
@@ -483,15 +481,16 @@
     attend(2, (2,), False, True)
     to_quad(2)
 
+    reduce(2)
     for which in range(2):
-        @pl.when(2 * (z % 4) + which != z)
-        def _():
-            rows = evict_rows(which, y)
-            copy(rows, rows, ezs.at[0], ezr.at[which], across).wait_recv()
-
-    @pl.when(jnp.logical_or(z == 0, z == NZ - 1))
-    def _():
-        evict_own().wait()
+        for g in range(2):
+            evict_z_wait(which, g)
+
+    for g in range(2):
+        for half in range(2):
+            @pl.when(evict_target(g, half) == z)
+            def _():
+                evict_own(g).wait()
 
     for which in range(2):
         for i in (1, 3):
@@ -499,7 +498,6 @@
 
     finish(0)
     finish(1)
-    reduce(2)
     for which, i in ((0, 1), (1, 3)):
         evict_y_wait(which, i)
         evict_relay(which, (y + NY - i) % NY).start()
@@ -549,8 +547,12 @@
         for there, k in ways:
             for each in final_copies(h, k, there):
                 each.wait_send()
-    step2(0, 1).wait_send()
-    step2(1, 2).wait_send()
+    step2().wait_send()
+    for i in range(3):
+        seat_copy(i).wait_send()
+    for i in range(4):
+        for k in (1, 2, 3):
+            quad_query(i, (seat + k) % 4).wait_send()
     for i in range(1, NXC):
         return1((xc + i) % NXC).wait_send()
     for i in (1, 3):
@@ -567,24 +569,11 @@
         for h in range(HEADS):
             for each in relay_copies(src, h, part):
                 each.wait_send()
-    for half in range(2):
-        @pl.when(z // 2 + 4 * half != z)
-        def _():
-            evict_z(half).wait_send()
-
-    def drain(block, carry):
-        for h in range(HEADS):
-            @pl.when(jnp.logical_and(block <= z, z < NZ - 1))
+    for g in range(2):
+        for half in range(2):
+            @pl.when(evict_target(g, half) != z)
             def _():
-                z_copy(block, h, 0).wait_send()
-
-            @pl.when(jnp.logical_and(block >= z, z > 0))
-            def _():
-                z_copy(block, h, 1).wait_send()
-
-        return carry
-
-    lax.fori_loop(0, NZ, drain, 0)
+                evict_z(g, half).wait_send()
 
 
 def attention(x, window, owner, oldest, slopes):
@@ -597,7 +586,7 @@
         out_shape=(
             jax.ShapeDtypeStruct((TOK, 2 * NXC * SHARE), F32),
             jax.ShapeDtypeStruct((2, CACHE, SHARE), BF),
-            jax.ShapeDtypeStruct((8, HD), F32),
+            jax.ShapeDtypeStruct((1, SHARE), F32),
         ),
         in_specs=[in_any] * 5,
         out_specs=(in_vmem, in_any, in_vmem),
@@ -612,7 +601,6 @@
             vm((NXC, OUT1, HD), BF),
             vm((NXC, OUT1, HD), BF),
             vm((2, 3, HALF, SHARE), F32),
-            vm((3, ROWS, SHARE), BF),
             vm((NZ, ROWS, SHARE), BF),
             vm((NY, HEADS, CACHE, HD), BF),
             vm((NY, HEADS, SUMS, CACHE), BF),
@@ -631,14 +619,14 @@
             vm((3, HALF, SHARE), BF),
             vm((NXC, BACK1, HD), BF),
             dma((NXC,)), dma((NXC,)),
-            dma((3,)), dma((3,)),
-            dma((2, NZ, HEADS)), dma((NZ, HEADS)),
+            dma(()), dma(()),
+            dma((3,)), dma((3,)), dma((4, 4)), dma((4, 4)),
             dma((NY, HEADS)), dma((NY, HEADS)), dma((NY, HEADS)), dma((NY, HEADS)),
             dma((2, HEADS)), dma((2, HEADS)), dma((2, HEADS)), dma((2, HEADS)),
             dma((NY,)), dma((NY,)), dma((2,)), dma((2,)),
             dma((HEADS, 4)), dma((HEADS, 4)), dma((HEADS, 4)), dma((HEADS, 4)),
             dma((HEADS, 3)), dma((2, HEADS, 2)), dma((HEADS, 3)), dma((2, HEADS, 2)),
-            dma((2,)), dma((2,)), dma((2, NY)), dma((2, NY)),
+            dma((2, 2)), dma((2, 2)), dma((2, NY)), dma((2, NY)),
             dma((2,)), dma((2,)),
             dma((NXC,)), dma((NXC,)), dma(()),
         ],
@@ -653,7 +641,7 @@
 
 def body(active_qkv, window_kv, slot_owner, oldest_slot, timestep, time_slopes, gate_table):
     combined, moved, flag = attention(active_qkv, window_kv, slot_owner, oldest_slot, time_slopes)
-    new_window = jnp.where(flag[0, 0] > 0, moved, window_kv)
+    new_window = jnp.where(flag[None] > 0, moved, window_kv)
     gate = lax.dynamic_slice_in_dim(gate_table, timestep[0], 1, 0)
     return ((gate * combined).astype(BF), new_window)
 

time: 108 us -> 102 us (0.944)
  Pallas kernels: 101 us -> 94.1 us
  other arithmetic: 2.75 us -> 4.7 us
  local copies, waits for them, and re-layouts: 1.23 us -> 0.04 us
    pallas_call x1, Pallas kernels: 101 us -> 94.1 us  [attention(): pl.pallas_call(kernel, out_shape=(jax.ShapeDtypeStruct((TOK, 2 * NXC * SH...]
    select_n x1, other arithmetic: 1.15 us -> 2.42 us  [body(): new_window = jnp.where(flag[None] > 0, moved, window_kv)]
    slice x1 -> x0, local copies, waits for them, and re-layouts: 1.18 us -> none  [body(): new_window = jnp.where(flag[0, 0] > 0, moved, window_kv)]
where the time goes in v4:
time: 102 us; the launch traced here: 101 us
  Pallas kernels  94.1 us (92%)
  other arithmetic  4.7 us (5%)
  between operations  2.07 us (2%)
    pallas_call x1, Pallas kernels, attention(): pl.pallas_call(kernel, out_shape=(jax.ShapeDtypeStruct((TOK, 2 * NXC * SH...  94.1 us
    select_n x1, other arithmetic, body(): new_window = jnp.where(flag[None] > 0, moved, window_kv)  2.42 us

profile of v4, /device:TPU:1, one launch (start us, length us, event | category | flops | bytes accessed | tf_op | source)
XLA Modules:
  0.0 100.9 jit_solution(9353835763797355417)
XLA Ops:
  0.6 0.0 copy-start
  2.0 0.0 copy-done
  2.1 0.0 copy-start.1
  2.1 94.1 %shard_map.86 = (f32[6,6144]{1,0:T(8,128)}, bf16[2,768,384]{2,1,0:T(8,128)(2,1)}, f32[1,384]{1,0:T(1,128)}) custom-call(bf16[3,6,6144]{2,1,0:T(8,128)(2,1)} %x_hbm.1, bf16[2,768,384]{2,1,0:T(8,128)(2,1)} %win_ref.1, s32[32]{0:T(128)} %owner_hbm.1, s32[1]{0:T(128)S(6)} %copy.9.oldest_hbm, f32[48]{0:T(128)} %slope_hbm.1), custom_call_target="tpu_custom_call" | custom-call | flops 4076863488 | bytes 4194304 | tf_op jit(solution)/shard_map/pallas_call | solution.py:584
  96.2 1.6 %multiply_convert_fusion = bf16[6,6144]{1,0:T(8,128)(2,1)} fusion(f32[6,6144]{1,0:T(8,128)} %get-tuple-element.5, f32[6144]{0:T(1024)S(1)} %bitcast.5), kind=kLoop, calls=%fused_computation.1 | loop fusion | flops 73728 | bytes 245760 | tf_op jit(solution)/shard_map/convert_element_type | solution.py:646
  97.8 0.7 compare_reduce_fusion
  98.4 0.0 copy-done.1
  98.5 2.4 %broadcast_select_fusion = bf16[2,768,384]{2,1,0:T(8,128)(2,1)} fusion(bf16[2,768,384]{2,1,0:T(8,128)(2,1)} %get-tuple-element.7, bf16[2,768,384]{2,1,0:T(8,128)(2,1)S(1)} %copy-done.1, pred[384]{0:T(512)(128)(4,1)S(1)} %compare_reduce_fusion), kind=kLoop, calls=%fused_computation | loop fusion | flops 589824 | bytes 3539328 | tf_op jit(solution)/shard_map/jit(_where)/select_n | solution.py:644
  (1 shorter events, 0.0 us)
Async XLA Ops:
  0.6 1.4 %copy-start = (f32[50,6144]{1,0:T(8,128)S(1)}, f32[50,6144]{1,0:T(8,128)}, u32[]{:S(2)}) copy-start(f32[50,6144]{1,0:T(8,128)} %param.13) | copy-start | bytes 3686404
  2.1 96.4 %copy-start.1 = (bf16[2,768,384]{2,1,0:T(8,128)(2,1)S(1)}, bf16[2,768,384]{2,1,0:T(8,128)(2,1)}, u32[]{:S(2)}) copy-start(bf16[2,768,384]{2,1,0:T(8,128)(2,1)} %win_ref.1) | copy-start | bytes 3538948

commit v5 on v4

--- a/solution.py
+++ b/solution.py
@@ -38,8 +38,8 @@
 
 
 def kernel(
-    x_hbm, win_ref, owner_hbm, oldest_hbm, slope_hbm, out_ref, moved_ref, flag_ref,
-    x_ref, vbuf, owner_ref, oldest_ref, slope_ref, in_sem,
+    x_hbm, win_ref, owner_hbm, oldest_hbm, time_hbm, slope_hbm, gate_hbm, out_ref, new_hbm,
+    x_ref, vbuf, gate_ref, owner_ref, oldest_ref, time_ref, slope_ref, moved_ref, in_sem, new_sem,
     pack32, packb, recv1, dense, qbuf, kbuf, vt, akv, vta, acc_ref, top_ref,
     so, sl, qo, ql, mo, ml, fo, fl, back, recv2,
     s1s, s1r, s2s, s2r, sas, sar, sbs, sbr, ks, kr, vs, vr, k2s, k2r, v2s, v2r, acs, acr, a2s, a2r,
@@ -78,7 +78,8 @@
         for i, (src, dst) in enumerate(
             [
                 (x_hbm, x_ref), (win_ref.at[1], vbuf), (owner_hbm, owner_ref),
-                (oldest_hbm, oldest_ref), (slope_hbm, slope_ref),
+                (oldest_hbm, oldest_ref), (slope_hbm, slope_ref), (time_hbm, time_ref),
+                (gate_hbm, gate_ref),
             ]
             + [(win_ref.at[0, :, h * HD : (h + 1) * HD], kbuf.at[y, h]) for h in range(HEADS)]
         )
@@ -174,7 +175,6 @@
         vta[h, HD:SUMS, :] = jnp.ones((SUMS - HD, PACK), BF)
     for load in loads[2:]:
         load.wait()
-    flag_ref[...] = jnp.full((1, SHARE), (owner_ref[me] == oldest_ref[0]).astype(F32))
 
     theirs = pl.ds(pl.multiple_of((1 - zh) * HALF, HALF), HALF)
     for h in range(HEADS):
@@ -231,7 +231,6 @@
     seat_copy(2).start()
     qbuf[z, mine, :] = dense[zh, 0].astype(BF)
     seat_copy(0).start()
-    pass_on(3)
 
     def step2():
         return copy(back.at[pl.ds(1, 2)], akv.at[y, :, mine, :], s2s, s2r, across_over)
@@ -241,6 +240,7 @@
     step2().start()
     for t in (1, 2):
         akv[y, t - 1, mine, :] = dense[zh, t].astype(BF)
+    pass_on(3)
 
     def a_copy(i):
         return copy(akv.at[y], akv.at[y], acs.at[i], acr.at[i], at(z, (y + i) % NY))
@@ -298,7 +298,7 @@
         rows = evict_rows(which, src)
         copy(rows, rows, eys.at[which, i], eyr.at[which, i], at(z, src)).wait_recv()
 
-    def attend(h, sources, start, stop):
+    def attend(h, active, sources, start, stop):
         cols = head_cols(h)
         q = qbuf[:, :, cols].reshape(NZ * ROWS, HD)
         slope = slope_ref[sp * HEADS + h] * LOG2E
@@ -310,7 +310,7 @@
             age = WIN - (slot + WIN) % WIN
             return kbuf[src, h, rows, :], vt.at[src, h, :, rows], slope * age.astype(F32)
 
-        chunks = [(akv[:, 0, :, cols].reshape(PACK, HD), vta.at[h], None)] if start else []
+        chunks = [(akv[:, 0, :, cols].reshape(PACK, HD), vta.at[h], None)] if active else []
         chunks += [window(i, part) for i in sources for part in range(2)]
         top, acc = (None, None) if start else (top_ref[0:1, :], acc_ref[...])
         ahead = lax.dot_general(chunks[0][0], q, NT, preferred_element_type=F32)
@@ -343,26 +343,32 @@
             so[h, j % 4, j // 4] = tokens[:, :HD].T[:ROWS].astype(BF)
             sl[h, j % 4, 4 * (j // 4) : 4 * (j // 4) + 4, :] = sums[:4, :HD]
 
-    def quad_copies(h, other):
-        dev = at(quad * 4 + other, y)
-        return (
-            copy(sl.at[h, other], ql.at[h, seat], qls.at[h, other], qlr.at[h, seat], dev),
-            copy(
-                so.at[h, other], qo.at[h, seat, :, pl.ds(0, ROWS), :], qos.at[h, other],
-                qor.at[h, seat], dev,
-            ),
-        )
-
-    def quad_wait(h, other):
+    def quad_lse(h, other):
+        return copy(
+            sl.at[h, other], ql.at[h, seat], qls.at[h, other], qlr.at[h, seat],
+            at(quad * 4 + other, y),
+        )
+
+    def quad_part(h, slot, other):
+        return copy(
+            so.at[h, other, slot], qo.at[h, seat, slot, pl.ds(0, ROWS), :],
+            qos.at[h, slot, other], qor.at[h, slot, seat], at(quad * 4 + other, y),
+        )
+
+    def quad_wait(h, slot, other):
+        part = qo.at[h, other, slot, pl.ds(0, ROWS), :]
+        copy(part, part, qos.at[h, slot, other], qor.at[h, slot, other], across).wait_recv()
+
+    def quad_lse_wait(h, other):
         part = ql.at[h, other]
         copy(part, part, qls.at[h, other], qlr.at[h, other], across).wait_recv()
-        part = qo.at[h, other, :, pl.ds(0, ROWS), :]
-        copy(part, part, qos.at[h, other], qor.at[h, other], across).wait_recv()
 
     def to_quad(h):
-        for i in (3, 2, 1):
-            for each in quad_copies(h, (seat + i) % 4):
-                each.start()
+        for i in (2, 1, 3):
+            quad_lse(h, (seat + i) % 4).start()
+        for slot in (quad, 1 - quad):
+            for i in (2, 1, 3):
+                quad_part(h, slot, (seat + i) % 4).start()
         ql[h, seat] = sl[h, seat]
         qo[h, seat, :, 0:ROWS, :] = so[h, seat]
 
@@ -385,10 +391,12 @@
     ways = ((2, 1), (1, 0), (0, 1))
 
     def reduce(h):
-        for i in (1, 2, 3):
-            quad_wait(h, (seat + i) % 4)
-        for k in (1, 0):
+        for i in (1, 3, 2):
+            quad_lse_wait(h, (seat + i) % 4)
+        for k in (0, 1):
             slot = (quad + k) % 2
+            for i in (1, 3, 2):
+                quad_wait(h, slot, (seat + i) % 4)
             row = pl.ds(slot * 4, 1)
             parts = [ql[h, i, row, :] for i in range(4)]
             whole = lse2(*parts)
@@ -433,21 +441,12 @@
     relay(0)
     seat_wait(1)
     pass_on(1)
+    for i in (1, 3):
+        k_copy(2, i).start()
     part = akv.at[y, :, theirs, :]
     copy(part, part, s2s, s2r, across).wait_recv()
     for i in (1, 3):
         a_copy(i).start()
-    for part, i in ((0, 1), (1, 3)):
-        a_wait(i)
-        a_relay((y + NY - i) % NY, part).start()
-    relay(1)
-    for i in (1, 3):
-        k_copy(2, i).start()
-        v_copy(2, i).start()
-    for i in (3, 0, 2, 1):
-        for k in (1, 2, 3):
-            quad_query_wait(i, (seat + k) % 4)
-
     for g in range(2):
         for half in range(2):
             @pl.when(evict_target(g, half) != z)
@@ -458,30 +457,35 @@
             def _():
                 evict_own(g).start()
 
+    relay(1)
+    for part, i in ((0, 1), (1, 3)):
+        a_wait(i)
+        a_relay((y + NY - i) % NY, part).start()
+    for i in (1, 3):
+        v_copy(2, i).start()
+    for i in (3, 0, 2, 1):
+        for k in (1, 2, 3):
+            quad_query_wait(i, (seat + k) % 4)
+
     for part in range(2):
         a_relay((y + 2) % NY, part).wait_recv()
     for h in range(HEADS):
         values = akv[:, 1, :, h * HD : (h + 1) * HD].reshape(PACK, HD)
         vta[h, 0:HD, :] = values.astype(F32).T.astype(BF)
-
-    def whole_head(h, carry):
+    for h in range(2):
         for part in range(2):
             relay_wait(h, part)
-        attend(h, (0, 1, 3, 2), True, True)
+        attend(h, True, (0, 1, 3, 2), True, True)
         to_quad(h)
-        return carry
-
-    lax.fori_loop(0, 2, whole_head, 0)
     relay(2)
-    attend(2, (0, 1, 3), True, False)
+    attend(2, True, (0, 1, 3), True, False)
     reduce(0)
-    reduce(1)
     for part in range(2):
         relay_wait(2, part)
-    attend(2, (2,), False, True)
+    attend(2, False, (2,), False, True)
     to_quad(2)
-
-    reduce(2)
+    reduce(1)
+
     for which in range(2):
         for g in range(2):
             evict_z_wait(which, g)
@@ -496,6 +500,7 @@
         for i in (1, 3):
             evict_y(which, i).start()
 
+    reduce(2)
     finish(0)
     finish(1)
     for which, i in ((0, 1), (1, 3)):
@@ -526,24 +531,39 @@
     for i in range(1, NXC):
         return1((xc + i) % NXC).start()
     recv2[xc] = packb[xc, 0:BACK1, :]
+    evict_y_wait(1, 1)
+    evict_y_wait(0, 3)
+    for which in range(2):
+        evict_relay(which, (y + 2) % NY).wait_recv()
+    for which, i in ((0, 1), (1, 3)):
+        evict_relay(which, (y + NY - i) % NY).wait_send()
+        for side in (1, 3):
+            evict_y(which, side).wait_send()
+    evicted = owner_ref[me] == oldest_ref[0]
+    for h in range(HEADS):
+        cols = slice(h * HD, (h + 1) * HD)
+        moved_ref[0, :, cols] = jnp.where(evicted, moved_ref[0, :, cols], kbuf[y, h])
+    moved_ref[1] = jnp.where(evicted, moved_ref[1], vbuf[...])
+    store = pltpu.make_async_copy(moved_ref, new_hbm, new_sem)
+    store.start()
     for i in range(1, NXC):
         return1_wait((xc + i) % NXC)
+    gate = gate_ref[pl.ds(time_ref[0], 1), :]
     for s in range(NXC):
         pack32[s, 0:BACK1, :] = recv2[s].astype(F32)
         for half in range(2):
             for h in range(HEADS):
                 row = (half * HEADS + h) * TOK
                 col = ((half * NXC + s) * HEADS + h) * HD
-                out_ref[:, col : col + HD] = pack32[s, row : row + TOK, :]
-
-    evict_y_wait(1, 1)
-    evict_y_wait(0, 3)
-    for which in range(2):
-        evict_relay(which, (y + 2) % NY).wait_recv()
+                rows = pack32[s, row : row + TOK, :] * gate[:, col : col + HD]
+                out_ref[:, col : col + HD] = rows.astype(BF)
+
+    store.wait()
     for h in range(HEADS):
         for i in (1, 2, 3):
-            for each in quad_copies(h, (seat + i) % 4):
-                each.wait_send()
+            quad_lse(h, (seat + i) % 4).wait_send()
+            for slot in range(2):
+                quad_part(h, slot, (seat + i) % 4).wait_send()
         for there, k in ways:
             for each in final_copies(h, k, there):
                 each.wait_send()
@@ -557,15 +577,12 @@
         return1((xc + i) % NXC).wait_send()
     for i in (1, 3):
         a_copy(i).wait_send()
-        for which in range(2):
-            evict_y(which, i).wait_send()
         for h in range(HEADS):
             k_copy(h, i).wait_send()
             v_copy(h, i).wait_send()
     for part, i in ((0, 1), (1, 3)):
         src = (y + NY - i) % NY
         a_relay(src, part).wait_send()
-        evict_relay(part, src).wait_send()
         for h in range(HEADS):
             for each in relay_copies(src, h, part):
                 each.wait_send()
@@ -576,7 +593,7 @@
                 evict_z(g, half).wait_send()
 
 
-def attention(x, window, owner, oldest, slopes):
+def attention(x, window, owner, oldest, timestep, slopes, gate_table):
     dma = pltpu.SemaphoreType.DMA
     vm = pltpu.VMEM
     in_vmem = pl.BlockSpec(memory_space=pltpu.VMEM)
@@ -584,19 +601,21 @@
     return pl.pallas_call(
         kernel,
         out_shape=(
-            jax.ShapeDtypeStruct((TOK, 2 * NXC * SHARE), F32),
+            jax.ShapeDtypeStruct((TOK, 2 * NXC * SHARE), BF),
             jax.ShapeDtypeStruct((2, CACHE, SHARE), BF),
-            jax.ShapeDtypeStruct((1, SHARE), F32),
         ),
-        in_specs=[in_any] * 5,
-        out_specs=(in_vmem, in_any, in_vmem),
+        in_specs=[pl.BlockSpec(memory_space=pltpu.HBM)] * 7,
+        out_specs=(in_vmem, in_any),
         scratch_shapes=[
             vm((3, TOK, 2 * NXC * SHARE), BF),
             vm((CACHE, SHARE), BF),
+            vm((50, 2 * NXC * SHARE), F32),
             pltpu.SMEM((NZ * NY,), jnp.int32),
             pltpu.SMEM((1,), jnp.int32),
+            pltpu.SMEM((1,), jnp.int32),
             pltpu.SMEM((2 * NXC * HEADS,), F32),
-            dma((8,)),
+            vm((2, CACHE, SHARE), BF),
+            dma((10,)), dma(()),
             vm((NXC, OUT1, HD), F32),
             vm((NXC, OUT1, HD), BF),
             vm((NXC, OUT1, HD), BF),
@@ -624,7 +643,7 @@
             dma((NY, HEADS)), dma((NY, HEADS)), dma((NY, HEADS)), dma((NY, HEADS)),
             dma((2, HEADS)), dma((2, HEADS)), dma((2, HEADS)), dma((2, HEADS)),
             dma((NY,)), dma((NY,)), dma((2,)), dma((2,)),
-            dma((HEADS, 4)), dma((HEADS, 4)), dma((HEADS, 4)), dma((HEADS, 4)),
+            dma((HEADS, 2, 4)), dma((HEADS, 2, 4)), dma((HEADS, 4)), dma((HEADS, 4)),
             dma((HEADS, 3)), dma((2, HEADS, 2)), dma((HEADS, 3)), dma((2, HEADS, 2)),
             dma((2, 2)), dma((2, 2)), dma((2, NY)), dma((2, NY)),
             dma((2,)), dma((2,)),
@@ -636,14 +655,53 @@
         cost_estimate=pl.CostEstimate(
             flops=4 * 3072 * 864 * SHARE, bytes_accessed=4 * 2**20, transcendentals=3072 * 864 * 3
         ),
-    )(x, window, owner, oldest, slopes)
+    )(x, window, owner, oldest, timestep, slopes, gate_table)
+
+
+def closing(attended_in, new_in, attended_out, new_out, attended, new, sem):
+    parts = [(attended_in, attended, attended_out)]
+    for half in range(2):
+        for part in range(2):
+            rows = pl.ds(part * PACK, PACK)
+            parts.append(
+                tuple(ref.at[half, rows, :] for ref in (new_in, new, new_out))
+            )
+    loads = [
+        pltpu.make_async_copy(src, held, sem.at[0, i]) for i, (src, held, _) in enumerate(parts)
+    ]
+    stores = [
+        pltpu.make_async_copy(held, dst, sem.at[1, i]) for i, (_, held, dst) in enumerate(parts)
+    ]
+    for load in loads:
+        load.start()
+    for load, store in zip(loads, stores):
+        load.wait()
+        store.start()
+    for store in stores:
+        store.wait()
+
+
+def close(attended, new):
+    in_hbm = pl.BlockSpec(memory_space=pltpu.HBM)
+    return pl.pallas_call(
+        closing,
+        out_shape=tuple(jax.ShapeDtypeStruct(a.shape, a.dtype) for a in (attended, new)),
+        in_specs=[in_hbm] * 2,
+        out_specs=[in_hbm] * 2,
+        scratch_shapes=[
+            pltpu.VMEM(attended.shape, attended.dtype),
+            pltpu.VMEM(new.shape, new.dtype),
+            pltpu.SemaphoreType.DMA((2, 5)),
+        ],
+        compiler_params=pltpu.CompilerParams(vmem_limit_bytes=60 * 1024 * 1024),
+    )(attended, new)
 
 
 def body(active_qkv, window_kv, slot_owner, oldest_slot, timestep, time_slopes, gate_table):
-    combined, moved, flag = attention(active_qkv, window_kv, slot_owner, oldest_slot, time_slopes)
-    new_window = jnp.where(flag[None] > 0, moved, window_kv)
-    gate = lax.dynamic_slice_in_dim(gate_table, timestep[0], 1, 0)
-    return ((gate * combined).astype(BF), new_window)
+    attended, new_window = attention(
+        active_qkv, window_kv, slot_owner, oldest_slot, timestep, time_slopes, gate_table
+    )
+    return close(attended, new_window)
 
 
 def solution(mesh):

time: 102 us -> 96.8 us (0.949)
  other arithmetic: 4.7 us -> 0 us
    select_n x1 -> x0, other arithmetic: 2.42 us -> none  [body(): new_window = jnp.where(flag[None] > 0, moved, window_kv)]
    pallas_call x0 -> x1, Pallas kernels: none -> 2.11 us  [close(): pl.pallas_call(closing, out_shape=tuple((jax.ShapeDtypeStruct(a.shape, a....]
    convert_element_type x1 -> x0, other arithmetic: 1.59 us -> none  [body(): return ((gate * combined).astype(BF), new_window)]
    pallas_call x1, Pallas kernels: 94.1 us -> 92.6 us  [attention(): pl.pallas_call(kernel, out_shape=(jax.ShapeDtypeStruct((TOK, 2 * NXC * SH...]
where the time goes in v5:
time: 96.8 us; the launch traced here: 96.6 us
  Pallas kernels  94.7 us (98%)
  between operations  1.93 us (2%)
    pallas_call x1, Pallas kernels, attention(): pl.pallas_call(kernel, out_shape=(jax.ShapeDtypeStruct((TOK, 2 * NXC * SH...  92.6 us
    pallas_call x1, Pallas kernels, close(): pl.pallas_call(closing, out_shape=tuple((jax.ShapeDtypeStruct(a.shape, a....  2.11 us

profile of v5, /device:TPU:1, one launch (start us, length us, event | category | flops | bytes accessed | tf_op | source)
XLA Modules:
  0.0 96.6 jit_solution(16495040398698755886)
XLA Ops:
  1.9 92.6 %shard_map.86 = (bf16[6,6144]{1,0:T(8,128)(2,1)}, bf16[2,768,384]{2,1,0:T(8,128)(2,1)}) custom-call(bf16[3,6,6144]{2,1,0:T(8,128)(2,1)} %x_hbm.1, bf16[2,768,384]{2,1,0:T(8,128)(2,1)} %win_ref.1, s32[32]{0:T(128)} %owner_hbm.1, s32[1]{0:T(128)S(6)} %copy.9.oldest_hbm, s32[1]{0:T(128)S(6)} %copy.10.time_hbm, f32[48]{0:T(128)} %slope_hbm.1, f32[50,6144]{1,0:T(8,128)} %gate_hbm.1), custom_call_target="tpu_custom_call" | custom-call | flops 4076863488 | bytes 4194304 | tf_op jit(solution)/shard_map/pallas_call | solution.py:601
  94.5 2.1 %shard_map.87 = (bf16[6,6144]{1,0:T(8,128)(2,1)}, bf16[2,768,384]{2,1,0:T(8,128)(2,1)}) custom-call(bf16[6,6144]{1,0:T(8,128)(2,1)} %get-tuple-element.4.attended_in, bf16[2,768,384]{2,1,0:T(8,128)(2,1)} %get-tuple-element.5.new_in), custom_call_target="tpu_custom_call" | custom-call | tf_op jit(solution)/shard_map/pallas_call | solution.py:686

commit v6 on v5

--- a/solution.py
+++ b/solution.py
@@ -108,9 +108,12 @@
             at(z, (y + i) % NY),
         )
 
-    def kv_wait(h, i):
+    def k_wait(h, i):
         src = (y + NY - i) % NY
         copy(kbuf.at[src, h], kbuf.at[src, h], ks.at[i, h], kr.at[i, h], at(z, src)).wait_recv()
+
+    def v_wait(h, i):
+        src = (y + NY - i) % NY
         rows = vt.at[src, h, pl.ds(0, HD), :]
         copy(rows, rows, vs.at[i, h], vr.at[i, h], at(z, src)).wait_recv()
 
@@ -126,11 +129,15 @@
             copy(values, values, v2s.at[part, h], v2r.at[part, h], dev),
         )
 
-    def relay(h):
+    def relay(h, keys=True, values=True):
         for part, i in ((0, 1), (1, 3)):
-            kv_wait(h, i)
-            for each in relay_copies((y + NY - i) % NY, h, part):
-                each.start()
+            on = relay_copies((y + NY - i) % NY, h, part)
+            if keys:
+                k_wait(h, i)
+                on[0].start()
+            if values:
+                v_wait(h, i)
+                on[1].start()
 
     def relay_wait(h, part):
         for each in relay_copies((y + 2) % NY, h, part):
@@ -468,22 +475,27 @@
             quad_query_wait(i, (seat + k) % 4)
 
     for part in range(2):
+        relay_wait(0, part)
+    attend(0, False, (0, 1, 3, 2), True, False)
+    for part in range(2):
         a_relay((y + 2) % NY, part).wait_recv()
     for h in range(HEADS):
         values = akv[:, 1, :, h * HD : (h + 1) * HD].reshape(PACK, HD)
         vta[h, 0:HD, :] = values.astype(F32).T.astype(BF)
-    for h in range(2):
-        for part in range(2):
-            relay_wait(h, part)
-        attend(h, True, (0, 1, 3, 2), True, True)
-        to_quad(h)
-    relay(2)
+    attend(0, True, (), False, True)
+    to_quad(0)
+    relay(2, values=False)
+    for part in range(2):
+        relay_wait(1, part)
+    attend(1, True, (0, 1, 3, 2), True, True)
+    to_quad(1)
+    relay(2, keys=False)
     attend(2, True, (0, 1, 3), True, False)
-    reduce(0)
     for part in range(2):
         relay_wait(2, part)
     attend(2, False, (2,), False, True)
     to_quad(2)
+    reduce(0)
     reduce(1)
 
     for which in range(2):

time: 96.8 us -> 94 us (0.971)
  Pallas kernels: 94.7 us -> 91.9 us
    pallas_call x1, Pallas kernels: 92.6 us -> 89.8 us  [attention(): pl.pallas_call(kernel, out_shape=(jax.ShapeDtypeStruct((TOK, 2 * NXC * SH...]
where the time goes in v6:
time: 94 us; the launch traced here: 93.9 us
  Pallas kernels  91.9 us (98%)
  between operations  1.93 us (2%)
    pallas_call x1, Pallas kernels, attention(): pl.pallas_call(kernel, out_shape=(jax.ShapeDtypeStruct((TOK, 2 * NXC * SH...  89.8 us
    pallas_call x1, Pallas kernels, close(): pl.pallas_call(closing, out_shape=tuple((jax.ShapeDtypeStruct(a.shape, a....  2.11 us

profile of v6, /device:TPU:1, one launch (start us, length us, event | category | flops | bytes accessed | tf_op | source)
XLA Modules:
  0.0 93.9 jit_solution(7736546063102861258)
XLA Ops:
  1.9 89.8 %shard_map.86 = (bf16[6,6144]{1,0:T(8,128)(2,1)}, bf16[2,768,384]{2,1,0:T(8,128)(2,1)}) custom-call(bf16[3,6,6144]{2,1,0:T(8,128)(2,1)} %x_hbm.1, bf16[2,768,384]{2,1,0:T(8,128)(2,1)} %win_ref.1, s32[32]{0:T(128)} %owner_hbm.1, s32[1]{0:T(128)S(6)} %copy.9.oldest_hbm, s32[1]{0:T(128)S(6)} %copy.10.time_hbm, f32[48]{0:T(128)} %slope_hbm.1, f32[50,6144]{1,0:T(8,128)} %gate_hbm.1), custom_call_target="tpu_custom_call" | custom-call | flops 4076863488 | bytes 4194304 | tf_op jit(solution)/shard_map/pallas_call | solution.py:613
  91.8 2.1 %shard_map.87 = (bf16[6,6144]{1,0:T(8,128)(2,1)}, bf16[2,768,384]{2,1,0:T(8,128)(2,1)}) custom-call(bf16[6,6144]{1,0:T(8,128)(2,1)} %get-tuple-element.4.attended_in, bf16[2,768,384]{2,1,0:T(8,128)(2,1)} %get-tuple-element.5.new_in), custom_call_target="tpu_custom_call" | custom-call | tf_op jit(solution)/shard_map/pallas_call | solution.py:698

commit v7 on v6

--- a/solution.py
+++ b/solution.py
@@ -233,20 +233,20 @@
         for k in (2, 1, 3):
             quad_query(i, (seat + k) % 4).start()
 
-    back[0] = dense[1 - zh, 0].astype(BF)
+    back[0] = dense[1 - zh, 0, 0:HALF].astype(BF)
     seat_copy(1).start()
     seat_copy(2).start()
-    qbuf[z, mine, :] = dense[zh, 0].astype(BF)
+    qbuf[z, mine, :] = dense[zh, 0, 0:HALF].astype(BF)
     seat_copy(0).start()
 
     def step2():
         return copy(back.at[pl.ds(1, 2)], akv.at[y, :, mine, :], s2s, s2r, across_over)
 
     for t in (1, 2):
-        back[t] = dense[1 - zh, t].astype(BF)
+        back[t] = dense[1 - zh, t, 0:HALF].astype(BF)
     step2().start()
     for t in (1, 2):
-        akv[y, t - 1, mine, :] = dense[zh, t].astype(BF)
+        akv[y, t - 1, mine, :] = dense[zh, t, 0:HALF].astype(BF)
     pass_on(3)
 
     def a_copy(i):
@@ -437,7 +437,7 @@
             weights = jnp.concatenate(
                 [spread(jnp.exp2(p - whole), zh * HALF, HALF) for p in parts], axis=1
             )
-            dense[half, 0, :, h * HD : (h + 1) * HD] = jnp.dot(
+            dense[half, 0, 0:HALF, h * HD : (h + 1) * HD] = jnp.dot(
                 weights, fo[half, h].reshape(2 * HD, HD), preferred_element_type=F32
             )
 
@@ -631,7 +631,7 @@
             vm((NXC, OUT1, HD), F32),
             vm((NXC, OUT1, HD), BF),
             vm((NXC, OUT1, HD), BF),
-            vm((2, 3, HALF, SHARE), F32),
+            vm((2, 3, HALF + 8, SHARE), F32),
             vm((NZ, ROWS, SHARE), BF),
             vm((NY, HEADS, CACHE, HD), BF),
             vm((NY, HEADS, SUMS, CACHE), BF),

time: 94 us -> 93.8 us (level)
  no operation moved by 1% of the time
where the time goes in v7:
time: 93.8 us; the launch traced here: 93.6 us
  Pallas kernels  91.7 us (98%)
  between operations  1.93 us (2%)
    pallas_call x1, Pallas kernels, attention(): pl.pallas_call(kernel, out_shape=(jax.ShapeDtypeStruct((TOK, 2 * NXC * SH...  89.6 us
    pallas_call x1, Pallas kernels, close(): pl.pallas_call(closing, out_shape=tuple((jax.ShapeDtypeStruct(a.shape, a....  2.11 us

profile of v7, /device:TPU:1, one launch (start us, length us, event | category | flops | bytes accessed | tf_op | source)
XLA Modules:
  0.0 93.6 jit_solution(7230555654000565210)
XLA Ops:
  1.9 89.6 %shard_map.86 = (bf16[6,6144]{1,0:T(8,128)(2,1)}, bf16[2,768,384]{2,1,0:T(8,128)(2,1)}) custom-call(bf16[3,6,6144]{2,1,0:T(8,128)(2,1)} %x_hbm.1, bf16[2,768,384]{2,1,0:T(8,128)(2,1)} %win_ref.1, s32[32]{0:T(128)} %owner_hbm.1, s32[1]{0:T(128)S(6)} %copy.9.oldest_hbm, s32[1]{0:T(128)S(6)} %copy.10.time_hbm, f32[48]{0:T(128)} %slope_hbm.1, f32[50,6144]{1,0:T(8,128)} %gate_hbm.1), custom_call_target="tpu_custom_call" | custom-call | flops 4076863488 | bytes 4194304 | tf_op jit(solution)/shard_map/pallas_call | solution.py:613
  91.5 2.1 %shard_map.87 = (bf16[6,6144]{1,0:T(8,128)(2,1)}, bf16[2,768,384]{2,1,0:T(8,128)(2,1)}) custom-call(bf16[6,6144]{1,0:T(8,128)(2,1)} %get-tuple-element.4.attended_in, bf16[2,768,384]{2,1,0:T(8,128)(2,1)} %get-tuple-element.5.new_in), custom_call_target="tpu_custom_call" | custom-call | tf_op jit(solution)/shard_map/pallas_call | solution.py:698
